TPU v7x, 32 devices: a whole 2x2x4 slice. The times are simulated.
32 devices in a mesh: lon: 8 (over z, core), lat: 2 (over y), dp: 2 (over x).
Axes of the slice: x: 2, y: 2, z: 4, core: 2. Of those that a mesh axis runs over, the one named last changes fastest.
Arguments:
- states: bfloat16 [2, 32, 512, 192], P('dp', 'lat', 'lon'), may hold values from -6 to 6
- cotangent: bfloat16 [2, 32, 512, 192], P('dp', 'lat', 'lon'), may hold values from -6 to 6
- kernel: bfloat16 [3, 3, 192, 192], replicated, may hold values from -0.15625 to 0.15625
- land_mask: int32 [32, 512], P('lat', 'lon'), may hold values 0 or 1
- ocean_tiles: int32 [2, 8, 3], P('lat', 'lon'), may hold values from 0 to 4, as said below
Outputs:
- output: bfloat16 [2, 32, 512, 192], P('dp', 'lat', 'lon')
- state_grad: bfloat16 [2, 32, 512, 192], P('dp', 'lat', 'lon')
- weight_grad: float32 [3, 3, 192, 192], replicated
Inputs may be any that keep to these rules, and one draw needn't show every extreme that they name: `ocean_tiles`: each device's 3 entries are distinct tile numbers of its block in increasing order, followed by the value 4 in unused slots; at least one slot is used, and some device uses all of them.
All inputs are finite; a program needn't handle non-finite values. No bound on the sum of `land_mask` on one device may be relied on, other than what follows from the above.
Results may differ from a plain program's by a relative error of at most 0.0049.
Values may be sent and summed in bfloat16 or wider, within the bound.
A program may use at most 64 MiB of HBM per device.

v0:
```python
from functools import partial
import math

import jax
import jax.numpy as jnp
from jax import lax
from jax.sharding import PartitionSpec as P

TS = 16


def with_halo(block, sides, width, periodic):
    for axis, dim in sides:
        count = lax.axis_size(axis)
        forward = [(i, i + 1) for i in range(count - 1)]
        if periodic:
            forward.append((count - 1, 0))
        backward = [(target, source) for source, target in forward]
        low = lax.ppermute(
            lax.slice_in_dim(block, block.shape[dim] - width, None, axis=dim), axis, forward
        )
        high = lax.ppermute(lax.slice_in_dim(block, 0, width, axis=dim), axis, backward)
        block = jnp.concatenate([low, block, high], axis=dim)
    return block


def from_partner(value, axis, distance):
    mask = 2**distance
    pairs = [(source, source ^ mask) for source in range(lax.axis_size(axis))]
    return lax.ppermute(value, axis, pairs)


def block_cut(block, row_start, col_start, size):
    return lax.dynamic_slice(
        block, (0, row_start, col_start, 0), (block.shape[0], size, size, block.shape[3])
    )


def plane_cut(plane, row_start, col_start, size):
    return lax.dynamic_slice(plane, (row_start, col_start), (size, size))


def body(states, cotangent, kernel, land_mask, ocean_tiles):
    batch_size, row_count, col_count, channels = states.shape
    tile_rows = row_count // TS
    tile_cols = col_count // TS
    per_device = tile_rows * tile_cols
    listed = ocean_tiles.reshape(-1)
    capacity = listed.shape[0]
    hit = jnp.any(listed[:, None] == jnp.arange(per_device, dtype=jnp.int32)[None, :], axis=0)
    table = hit.reshape(tile_rows, tile_cols).astype(jnp.float32)
    keep_cells = land_mask.astype(jnp.float32) * jnp.repeat(
        jnp.repeat(table, TS, axis=0), TS, axis=1
    )
    keep_full = keep_cells[None, :, :, None]
    masked = jnp.where(keep_full > 0, states, jnp.zeros_like(states))
    lon_ext = with_halo(masked, (("lon", 2),), 1, True)
    lat_ext = with_halo(lon_ext, (("lat", 1),), 1, False)
    northmost = lax.axis_index("lat") == lax.axis_size("lat") - 1
    lon_count = lax.axis_size("lon")
    moving = lon_ext[:, row_count - 1]
    for bit_number in range(lon_count.bit_length() - 1):
        moving = from_partner(moving, "lon", bit_number)
    north = jnp.flip(moving, axis=1)
    padded = lat_ext.at[:, row_count + 1].set(
        jnp.where(northmost, north, lat_ext[:, row_count + 1])
    )
    slot_tile = jnp.minimum(listed, per_device - 1)
    valid = (listed < per_device).astype(jnp.float32)
    row_start = slot_tile // tile_cols * TS
    col_start = slot_tile % tile_cols * TS
    windows = jax.vmap(partial(block_cut, size=TS + 2), in_axes=(None, 0, 0))(
        padded, row_start, col_start
    )
    keep_tiles = jax.vmap(partial(plane_cut, size=TS), in_axes=(None, 0, 0))(
        keep_cells, row_start, col_start
    )
    keep_tiles = (keep_tiles * valid[:, None, None])[:, None, :, :, None]
    upstream = jax.vmap(partial(block_cut, size=TS), in_axes=(None, 0, 0))(
        cotangent, row_start, col_start
    )
    preact = jnp.zeros((capacity, batch_size, TS, TS, channels), jnp.float32)
    for row_shift in range(3):
        for col_shift in range(3):
            preact = preact + jnp.einsum(
                "sbyxc,cd->sbyxd",
                windows[:, :, row_shift : row_shift + TS, col_shift : col_shift + TS],
                kernel[row_shift, col_shift],
                preferred_element_type=jnp.float32,
            )
    sigmoid_h = jax.nn.sigmoid(preact)
    out_tiles = (keep_tiles * preact * sigmoid_h).astype(jnp.bfloat16)
    slope = sigmoid_h * (1.0 + preact * (1.0 - sigmoid_h))
    grad_pre = (keep_tiles * upstream.astype(jnp.float32) * slope).astype(jnp.bfloat16)
    target = jnp.where(listed < per_device, listed, per_device)
    holder = (
        jnp.zeros((per_device + 1, batch_size, TS, TS, channels), jnp.bfloat16)
        .at[target]
        .set(out_tiles)
    )
    holder = holder[:per_device].reshape(tile_rows, tile_cols, batch_size, TS, TS, channels)
    output = holder.transpose(2, 0, 3, 1, 4, 5).reshape(batch_size, row_count, col_count, channels)
    kernel_terms = []
    grad_windows = jnp.zeros((capacity, batch_size, TS + 2, TS + 2, channels), jnp.float32)
    for row_shift in range(3):
        for col_shift in range(3):
            piece = windows[:, :, row_shift : row_shift + TS, col_shift : col_shift + TS]
            kernel_terms.append(
                jnp.einsum("sbyxc,sbyxd->cd", piece, grad_pre, preferred_element_type=jnp.float32)
            )
            backed = jnp.einsum(
                "sbyxd,cd->sbyxc",
                grad_pre,
                kernel[row_shift, col_shift],
                preferred_element_type=jnp.float32,
            )
            grad_windows = grad_windows.at[
                :, :, row_shift : row_shift + TS, col_shift : col_shift + TS
            ].add(backed)
    partial_kernel = jnp.stack(kernel_terms).reshape(3, 3, channels, channels)

    def place(slot, total):
        spot = (0, row_start[slot], col_start[slot], 0)
        current = lax.dynamic_slice(total, spot, grad_windows.shape[1:])
        return lax.dynamic_update_slice(total, current + grad_windows[slot], spot)

    grad_pad = lax.fori_loop(
        0,
        capacity,
        place,
        jnp.zeros((batch_size, row_count + 2, col_count + 2, channels), jnp.float32),
    )
    north_grad = grad_pad[:, row_count + 1]
    moving_grad = north_grad
    for bit_number in range(lon_count.bit_length() - 1):
        moving_grad = from_partner(moving_grad.astype(jnp.bfloat16), "lon", bit_number).astype(
            moving_grad.dtype
        )
    returned = jnp.flip(moving_grad, axis=1)
    edges = jnp.concatenate([grad_pad[:, 0:1], grad_pad[:, row_count + 1 : row_count + 2]], axis=1)
    arrived = with_halo(edges.astype(jnp.bfloat16), (("lat", 1),), 1, False).astype(edges.dtype)
    unfolded = grad_pad[:, 1 : row_count + 1]
    unfolded = unfolded.at[:, 0].add(arrived[:, 0])
    unfolded = unfolded.at[:, row_count - 1].add(
        arrived[:, 3] + jnp.where(northmost, returned, jnp.zeros_like(returned))
    )
    sides = jnp.concatenate(
        [unfolded[:, :, 0:1], unfolded[:, :, col_count + 1 : col_count + 2]], axis=2
    )
    side_back = with_halo(sides, (("lon", 2),), 1, True)
    inner = unfolded[:, :, 1 : col_count + 1]
    inner = inner.at[:, :, 0].add(side_back[:, :, 0])
    inner = inner.at[:, :, col_count - 1].add(side_back[:, :, 3])
    state_grad = jnp.where(keep_full > 0, inner, jnp.zeros_like(inner)).astype(jnp.bfloat16)
    summed = lax.psum(partial_kernel, ("lon", "lat", "dp"))
    flat_count = (
        batch_size * lax.axis_size("dp") * row_count * lax.axis_size("lat") * col_count * lon_count
    )
    weight_grad = summed / math.sqrt(flat_count)
    return (output, state_grad, weight_grad)


def solution(mesh):
    in_specs = (
        P("dp", "lat", "lon", None),
        P("dp", "lat", "lon", None),
        P(),
        P("lat", "lon"),
        P("lat", "lon", None),
    )
    out_specs = (P("dp", "lat", "lon", None), P("dp", "lat", "lon", None), P())
    return jax.shard_map(body, mesh=mesh, in_specs=in_specs, out_specs=out_specs, check_vma=False)
```

profile of v0, /device:TPU:1, one launch (start us, length us, event | category | flops | bytes accessed | tf_op | source)
XLA Modules:
  0.0 278.5 jit_solution(4870413857106391396)
XLA Ops:
  9.0 1.4 copy_select_fusion
  10.4 2.7 collective-permute-start
  15.2 3.9 %while.29 = (s32[]{:T(128)}, f32[16,64]{1,0:T(8,128)S(1)}, s32[3,2]{0,1:T(2,128)S(1)}, f32[3,16,16]{2,1,0:T(8,128)S(1)}, s32[]{:T(128)}) while((s32[]{:T(128)}, f32[16,64]{1,0:T(8,128)S(1)}, s32[3,2]{0,1:T(2,128)S(1)}, f32[3,16,16]{2,1,0:T(8,128)S(1)}, s32[]{:T(128)}) %tuple.121), condition=%wide.while_cond.14, body=%wide.while_body.14.sunk | while | flops 2 | bytes 16489 | solution.py:40
  19.2 1.4 and_reduce_fusion
  20.7 2.0 collective-permute-start.4
  23.3 3.6 %collective-permute-start.2 = (bf16[1,1,66,192]{3,1,0,2:T(2,128)(2,1)S(1)}, bf16[1,1,66,192]{3,1,0,2:T(2,128)(2,1)S(1)}, u32[]{:S(2)}, u32[]{:S(2)}) collective-permute-start(bf16[1,1,66,192]{3,1,0,2:T(2,128)(2,1)S(1)} %get-tuple-element.330), channel_id=1, source_target_pairs={{0,2},{1,3},{4,6},{5,7},{8,10},{9,11},{12,14},{13,15},{16,18},{17,... | collective-permute-start | bytes 76040 | tf_op jit(solution)/shard_map/ppermute | solution.py:19
  26.9 1.3 collective-permute-start.3
  29.2 1.3 gather_fusion.1
  32.8 3.4 %collective-permute-done.6 = bf16[1,66,192]{2,0,1:T(2,128)(2,1)S(1)} collective-permute-done((bf16[1,66,192]{2,0,1:T(2,128)(2,1)S(1)}, bf16[1,66,192]{2,0,1:T(2,128)(2,1)S(1)}, u32[]{:S(2)}, u32[]{:S(2)}) %collective-permute-start.6) | collective-permute-done | bytes 25376 | tf_op jit(solution)/shard_map/ppermute | solution.py:30
  36.3 2.1 scatter.12
  42.6 1.0 fusion.19
  45.4 3.3 %fusion = f32[3,1,16,16,192]{4,3,2,0,1:T(8,128)} fusion(bf16[3,16,16,192]{3,2,1,0:T(8,128)(2,1)S(1)} %get-tuple-element.328, s32[]{:T(128)} %bitcast.53, s32[]{:T(128)} %bitcast.54, f32[3,1,16,16,192]{4,3,2,0,1:T(8,128)S(1)} %convolution_bitcast_fusion.8, bf16[3,3,192,192]{3,2,1,0:T(8,128)(2,1)} %param.37), kind=kOutput, calls=%fused_computation.23 | convolution fusion | flops 56770560 | bytes 1573888 | tf_op jit(solution)/shard_map/sbyxd,cd->sbyxc/dot_general | solution.py:111
  48.8 5.2 %scatter-add.45 = f32[3,1,18,18,192]{4,3,2,0,1:T(8,128)S(1)} dynamic-update-slice(f32[3,1,18,18,192]{4,3,2,0,1:T(8,128)S(1)} %scatter-add.44, f32[3,1,16,16,192]{4,3,2,0,1:T(8,128)} %fusion, s32[]{:T(128)} %constant.480.clone.1, s32[]{:T(128)} %constant.480.clone.1, s32[]{:T(128)} %bitcast.53, s32[]{:T(128)} %bitcast.54, s32[]{:T(128)} %constant.480.clone.1) | dynamic-update-slice | bytes 1179652 | tf_op jit(solution)/shard_map/scatter-add | solution.py:119
  54.0 3.0 %fusion.2 = f32[3,1,16,16,192]{4,3,2,0,1:T(8,128)} fusion(bf16[3,16,16,192]{3,2,1,0:T(8,128)(2,1)S(1)} %get-tuple-element.328, f32[3,1,18,18,192]{4,3,2,0,1:T(8,128)S(1)} %scatter-add.45, s32[]{:T(128)} %bitcast.58, s32[]{:T(128)} %bitcast.59, pred[]{:T(512)} %and_reduce_fusion, bf16[3,3,192,192]{3,2,1,0:T(8,128)(2,1)S(1)} %copy-done.2), kind=kOutput, calls=%fused_computation.25 | convolution fusion | flops 56918016 | bytes 1867785 | tf_op jit(solution)/shard_map/sbyxd,cd->sbyxc/dot_general | solution.py:111
  57.0 5.1 %scatter-add.46 = f32[3,1,18,18,192]{4,3,2,0,1:T(8,128)S(1)} dynamic-update-slice(f32[3,1,18,18,192]{4,3,2,0,1:T(8,128)S(1)} %scatter-add.45, f32[3,1,16,16,192]{4,3,2,0,1:T(8,128)} %fusion.2, s32[]{:T(128)} %constant.480.clone.1, s32[]{:T(128)} %constant.480.clone.1, s32[]{:T(128)} %bitcast.58, s32[]{:T(128)} %bitcast.59, s32[]{:T(128)} %constant.480.clone.1) | dynamic-update-slice | bytes 1179652 | tf_op jit(solution)/shard_map/scatter-add | solution.py:119
  62.4 1.2 fusion.5
  63.6 3.8 %scatter-add.50 = f32[3,1,18,18,192]{4,3,2,0,1:T(8,128)S(1)} dynamic-update-slice(f32[3,1,18,18,192]{4,3,2,0,1:T(8,128)S(1)} %fusion.4, f32[3,1,16,16,192]{4,3,2,0,1:T(8,128)} %fusion.5, s32[]{:T(128)} %constant.480.clone.1, s32[]{:T(128)} %constant.480.clone.1, s32[]{:T(128)} %constant.484.clone.1, s32[]{:T(128)} %constant.484.clone.1, s32[]{:T(128)} %constant.480.clone.1) | dynamic-update-slice | bytes 1179652 | tf_op jit(solution)/shard_map/scatter-add | solution.py:119
  67.4 1.2 fusion.6
  68.6 3.8 %scatter-add.51 = f32[3,1,18,18,192]{4,3,2,0,1:T(8,128)S(1)} dynamic-update-slice(f32[3,1,18,18,192]{4,3,2,0,1:T(8,128)S(1)} %scatter-add.50, f32[3,1,16,16,192]{4,3,2,0,1:T(8,128)} %fusion.6, s32[]{:T(128)} %constant.480.clone.1, s32[]{:T(128)} %constant.480.clone.1, s32[]{:T(128)} %constant.484.clone.1, s32[]{:T(128)} %constant.485.clone.1, s32[]{:T(128)} %constant.480.clone.1) | dynamic-update-slice | bytes 1179652 | tf_op jit(solution)/shard_map/scatter-add | solution.py:119
  72.8 1.2 fusion.9
  74.0 3.8 %scatter-add.55 = f32[3,1,18,18,192]{4,3,2,0,1:T(8,128)S(1)} dynamic-update-slice(f32[3,1,18,18,192]{4,3,2,0,1:T(8,128)S(1)} %fusion.8, f32[3,1,16,16,192]{4,3,2,0,1:T(8,128)} %fusion.9, s32[]{:T(128)} %constant.480.clone.1, s32[]{:T(128)} %constant.480.clone.1, s32[]{:T(128)} %constant.485.clone.1, s32[]{:T(128)} %constant.484.clone.1, s32[]{:T(128)} %constant.480.clone.1) | dynamic-update-slice | bytes 1179652 | tf_op jit(solution)/shard_map/scatter-add | solution.py:119
  77.8 1.2 fusion.10
  79.0 3.8 %scatter-add.56 = f32[3,1,18,18,192]{4,3,2,0,1:T(8,128)S(1)} dynamic-update-slice(f32[3,1,18,18,192]{4,3,2,0,1:T(8,128)S(1)} %scatter-add.55, f32[3,1,16,16,192]{4,3,2,0,1:T(8,128)} %fusion.10, s32[]{:T(128)} %constant.480.clone.1, s32[]{:T(128)} %constant.480.clone.1, s32[]{:T(128)} %constant.485.clone.1, s32[]{:T(128)} %constant.485.clone.1, s32[]{:T(128)} %constant.480.clone.1) | dynamic-update-slice | bytes 1179652 | tf_op jit(solution)/shard_map/scatter-add | solution.py:119
  82.8 1.2 broadcast_in_dim.57
  84.0 21.7 %while.28 = (s32[]{:T(128)}, f32[1,18,66,192]{3,2,1,0:T(8,128)}, s32[3]{0:T(128)S(1)}, f32[3,1,18,18,192]{4,3,2,1,0:T(8,128)S(1)}, s32[]{:T(128)}, /*index=5*/s32[]{:T(128)}, s32[]{:T(128)}) while((s32[]{:T(128)}, f32[1,18,66,192]{3,2,1,0:T(8,128)}, s32[3]{0:T(128)S(1)}, f32[3,1,18,18,192]{4,3,2,1,0:T(8,128)S(1)}, s32[]{:T(128)}, ...), condition=%wide.region_4.5_spmd, body=%wide.region_3.4_spmd.sunk | while | flops 62213 | bytes 1244303 | solution.py:127
  86.6 1.2 bitcast_add_fusion.2
  87.8 3.6 %dynamic_update_slice.9 = f32[1,18,66,192]{3,2,1,0:T(8,128)} dynamic-update-slice(f32[1,18,66,192]{3,2,1,0:T(8,128)} %get-tuple-element.415, f32[1,18,18,192]{3,2,1,0:T(8,128)S(1)} %bitcast_add_fusion.2, s32[]{:T(128)} %constant.480.clone.1..sunk, s32[]{:T(128)} %constant.480.clone.1..sunk, s32[]{:T(128)S(6)} %select_n.220, s32[]{:T(128)} %constant.480.clone.1..sunk) | dynamic-update-slice | bytes 497668 | tf_op jit(solution)/shard_map/while/body/eval_jaxpr/dynamic_update_slice | solution.py:125
  94.1 1.2 bitcast_add_fusion.2
  95.2 3.6 %dynamic_update_slice.9 = f32[1,18,66,192]{3,2,1,0:T(8,128)} dynamic-update-slice(f32[1,18,66,192]{3,2,1,0:T(8,128)} %get-tuple-element.415, f32[1,18,18,192]{3,2,1,0:T(8,128)S(1)} %bitcast_add_fusion.2, s32[]{:T(128)} %constant.480.clone.1..sunk, s32[]{:T(128)} %constant.480.clone.1..sunk, s32[]{:T(128)S(6)} %select_n.220, s32[]{:T(128)} %constant.480.clone.1..sunk) | dynamic-update-slice | bytes 497668 | tf_op jit(solution)/shard_map/while/body/eval_jaxpr/dynamic_update_slice | solution.py:125
  101.5 1.1 bitcast_add_fusion.2
  102.7 3.0 %dynamic_update_slice.9 = f32[1,18,66,192]{3,2,1,0:T(8,128)} dynamic-update-slice(f32[1,18,66,192]{3,2,1,0:T(8,128)} %get-tuple-element.415, f32[1,18,18,192]{3,2,1,0:T(8,128)S(1)} %bitcast_add_fusion.2, s32[]{:T(128)} %constant.480.clone.1..sunk, s32[]{:T(128)} %constant.480.clone.1..sunk, s32[]{:T(128)S(6)} %select_n.220, s32[]{:T(128)} %constant.480.clone.1..sunk) | dynamic-update-slice | bytes 497668 | tf_op jit(solution)/shard_map/while/body/eval_jaxpr/dynamic_update_slice | solution.py:125
  106.7 1.3 collective-permute-start.8
  108.0 2.4 collective-permute-start.9
  110.4 1.0 fusion.18
  112.3 1.0 fusion.16
  113.3 1.0 fusion.15
  114.3 1.0 fusion.14
  116.2 1.0 fusion.12
  117.3 4.5 %collective-permute-start.7 = (bf16[1,1,66,192]{3,1,2,0:T(2,128)(2,1)S(1)}, bf16[1,1,66,192]{3,1,2,0:T(2,128)(2,1)S(1)}, u32[]{:S(2)}, u32[]{:S(2)}) collective-permute-start(bf16[1,1,66,192]{3,1,2,0:T(2,128)(2,1)S(1)} %copy.142), channel_id=1, source_target_pairs={{0,2},{1,3},{4,6},{5,7},{8,10},{9,11},{12,14},{13,15},{16,18},{17,... | collective-permute-start | bytes 76040 | tf_op jit(solution)/shard_map/ppermute | solution.py:19
  122.7 2.3 collective-permute-done.10
  125.0 1.2 collective-permute-start.11
  126.5 2.9 %scatter-add.59 = f32[1,16,66,192]{3,1,0,2:T(8,128)S(1)} dynamic-update-slice(f32[1,16,66,192]{3,1,0,2:T(8,128)S(1)} %slice.690, f32[1,1,66,192]{3,1,0,2:T(1,128)S(1)} %fusion.64, s32[]{:T(128)} %constant.480.clone.1, s32[]{:T(128)} %constant.480.clone.1, s32[]{:T(128)} %constant.480.clone.1, s32[]{:T(128)} %constant.480.clone.1) | dynamic-update-slice | bytes 101380 | tf_op jit(solution)/shard_map/scatter-add | solution.py:143
  130.2 2.9 %scatter-add.60 = f32[1,16,66,192]{3,1,0,2:T(8,128)S(1)} dynamic-update-slice(f32[1,16,66,192]{3,1,0,2:T(8,128)S(1)} %scatter-add.59, f32[1,1,66,192]{3,1,0,2:T(1,128)S(1)} %slice_add_fusion, s32[]{:T(128)} %constant.480.clone.1, s32[]{:T(128)} %constant.498.clone.1, s32[]{:T(128)} %constant.480.clone.1, s32[]{:T(128)} %constant.480.clone.1) | dynamic-update-slice | bytes 101380 | tf_op jit(solution)/shard_map/scatter-add | solution.py:144
  133.1 2.1 collective-permute-start.12
  135.1 1.0 fusion.11
  137.4 2.9 %collective-permute-done.13 = f32[1,16,1,192]{3,1,0,2:T(8,128)S(1)} collective-permute-done((f32[1,16,1,192]{3,1,0,2:T(8,128)S(1)}, f32[1,16,1,192]{3,1,0,2:T(8,128)S(1)}, u32[]{:S(2)}, u32[]{:S(2)}) %collective-permute-start.13) | collective-permute-done | bytes 12320 | tf_op jit(solution)/shard_map/ppermute | solution.py:22
  141.5 127.4 %all-reduce.3.cloned.1.call-done = f32[3,3,192,192]{3,2,1,0:T(8,128)} async-done(((f32[3,3,192,192]{3,2,1,0:T(8,128)}), f32[3,3,192,192]{3,2,1,0:T(8,128)}) %all-reduce.3.cloned.1.call-update) | async-done | bytes 1327120 | tf_op jit(solution)/shard_map/psum | solution.py:155
  268.9 2.8 %broadcast_multiply_fusion = f32[3,3,192,192]{3,2,1,0:T(8,128)} fusion(f32[3,3,192,192]{3,2,1,0:T(8,128)} %all-reduce.3.cloned.1.call-done), kind=kLoop, calls=%fused_computation.53 | loop fusion | flops 331776 | bytes 2654208 | tf_op jit(solution)/shard_map/div | solution.py:159
  (103 shorter events, 28.0 us)
Async XLA Ops:
  7.2 21.7 %copy-start.4 = (bf16[1,16,64,192]{3,2,1,0:T(8,128)(2,1)S(1)}, bf16[1,16,64,192]{3,2,1,0:T(8,128)(2,1)}, u32[]{:S(2)}) copy-start(bf16[1,16,64,192]{3,2,1,0:T(8,128)(2,1)} %param.36) | copy-start | bytes 1179652
  7.2 261.7 %all-reduce.3.cloned.1.call-start = ((), (), s32[]{:S(2)}) async-start(), calls=%async_computation | async-start | bytes 3538944 | tf_op jit(solution)/shard_map/psum | solution.py:155
  10.4 10.2 %collective-permute-start = (bf16[1,16,1,192]{3,1,0,2:T(8,128)(2,1)S(1)}, bf16[1,16,1,192]{3,1,0,2:T(8,128)(2,1)S(1)}, u32[]{:S(2)}, u32[]{:S(2)}) collective-permute-start(bf16[1,16,1,192]{3,1,0,2:T(8,128)(2,1)S(1)} %get-tuple-element.332), channel_id=1, source_target_pairs={{0,4},{4,8},{8,12},{12,16},{16,20},{20,24},{24,28},{28,0},{1,5},{5... | collective-permute-start | bytes 18440 | tf_op jit(solution)/shard_map/ppermute | solution.py:19
  13.1 7.5 %collective-permute-start.1 = (bf16[1,16,1,192]{3,1,0,2:T(8,128)(2,1)S(1)}, bf16[1,16,1,192]{3,1,0,2:T(8,128)(2,1)S(1)}, u32[]{:S(2)}, u32[]{:S(2)}) collective-permute-start(bf16[1,16,1,192]{3,1,0,2:T(8,128)(2,1)S(1)} %get-tuple-element.333), channel_id=1, source_target_pairs={{4,0},{8,4},{12,8},{16,12},{20,16},{24,20},{28,24},{0,28},{5,1},{9... | collective-permute-start | bytes 18440 | tf_op jit(solution)/shard_map/ppermute | solution.py:22
  20.7 7.5 %collective-permute-start.4 = (bf16[1,66,192]{2,0,1:T(2,128)(2,1)S(1)}, bf16[1,66,192]{2,0,1:T(2,128)(2,1)S(1)}, u32[]{:S(2)}, u32[]{:S(2)}) collective-permute-start(bf16[1,66,192]{2,0,1:T(2,128)(2,1)S(1)} %bitcast.348), channel_id=1, source_target_pairs={{0,4},{4,0},{8,12},{12,8},{16,20},{20,16},{24,28},{28,24},{1,5},{5... | collective-permute-start | bytes 76040 | tf_op jit(solution)/shard_map/ppermute | solution.py:30
  23.3 9.0 %collective-permute-start.2 = (bf16[1,1,66,192]{3,1,0,2:T(2,128)(2,1)S(1)}, bf16[1,1,66,192]{3,1,0,2:T(2,128)(2,1)S(1)}, u32[]{:S(2)}, u32[]{:S(2)}) collective-permute-start(bf16[1,1,66,192]{3,1,0,2:T(2,128)(2,1)S(1)} %get-tuple-element.330), channel_id=1, source_target_pairs={{0,2},{1,3},{4,6},{5,7},{8,10},{9,11},{12,14},{13,15},{16,18},{17,... | collective-permute-start | bytes 76040 | tf_op jit(solution)/shard_map/ppermute | solution.py:19
  26.9 5.4 %collective-permute-start.3 = (bf16[1,1,66,192]{3,1,0,2:T(2,128)(2,1)S(1)}, bf16[1,1,66,192]{3,1,0,2:T(2,128)(2,1)S(1)}, u32[]{:S(2)}, u32[]{:S(2)}) collective-permute-start(bf16[1,1,66,192]{3,1,0,2:T(2,128)(2,1)S(1)} %get-tuple-element.331), channel_id=1, source_target_pairs={{2,0},{3,1},{6,4},{7,5},{10,8},{11,9},{14,12},{15,13},{18,16},{19,... | collective-permute-start | bytes 76040 | tf_op jit(solution)/shard_map/ppermute | solution.py:22
  28.2 3.2 %collective-permute-start.5 = (bf16[1,66,192]{2,0,1:T(2,128)(2,1)S(1)}, bf16[1,66,192]{2,0,1:T(2,128)(2,1)S(1)}, u32[]{:S(2)}, u32[]{:S(2)}) collective-permute-start(bf16[1,66,192]{2,0,1:T(2,128)(2,1)S(1)} %collective-permute-done.4), channel_id=1, source_target_pairs={{0,8},{4,12},{8,0},{12,4},{16,24},{20,28},{24,16},{28,20},{1,9},{5... | collective-permute-start | bytes 76040 | tf_op jit(solution)/shard_map/ppermute | solution.py:30
  31.4 4.8 %collective-permute-start.6 = (bf16[1,66,192]{2,0,1:T(2,128)(2,1)S(1)}, bf16[1,66,192]{2,0,1:T(2,128)(2,1)S(1)}, u32[]{:S(2)}, u32[]{:S(2)}) collective-permute-start(bf16[1,66,192]{2,0,1:T(2,128)(2,1)S(1)} %collective-permute-done.5), channel_id=1, source_target_pairs={{0,16},{4,20},{8,24},{12,28},{16,0},{20,4},{24,8},{28,12},{1,17},{... | collective-permute-start | bytes 76040 | tf_op jit(solution)/shard_map/ppermute | solution.py:30
  32.8 6.3 %copy-start.1 = (bf16[3,3,192,192]{3,2,1,0:T(8,128)(2,1)S(1)}, bf16[3,3,192,192]{3,2,1,0:T(8,128)(2,1)}, u32[]{:S(2)}) copy-start(bf16[3,3,192,192]{3,2,1,0:T(8,128)(2,1)} %param.37) | copy-start | bytes 1990660
  40.7 1.0 copy-start.5
  48.8 5.2 %copy-start.2 = (bf16[3,3,192,192]{3,2,1,0:T(8,128)(2,1)S(1)}, bf16[3,3,192,192]{3,2,1,0:T(8,128)(2,1)}, u32[]{:S(2)}) copy-start(bf16[3,3,192,192]{3,2,1,0:T(8,128)(2,1)} %param.37) | copy-start | bytes 1990660
  106.7 19.5 %collective-permute-start.8 = (bf16[1,1,66,192]{3,1,2,0:T(2,128)(2,1)S(1)}, bf16[1,1,66,192]{3,1,2,0:T(2,128)(2,1)S(1)}, u32[]{:S(2)}, u32[]{:S(2)}) collective-permute-start(bf16[1,1,66,192]{3,1,2,0:T(2,128)(2,1)S(1)} %copy.141), channel_id=1, source_target_pairs={{2,0},{3,1},{6,4},{7,5},{10,8},{11,9},{14,12},{15,13},{18,16},{19,... | collective-permute-start | bytes 76040 | tf_op jit(solution)/shard_map/ppermute | solution.py:22
  108.0 13.8 %collective-permute-start.9 = (bf16[1,66,192]{2,0,1:T(2,128)(2,1)S(1)}, bf16[1,66,192]{2,0,1:T(2,128)(2,1)S(1)}, u32[]{:S(2)}, u32[]{:S(2)}) collective-permute-start(bf16[1,66,192]{2,0,1:T(2,128)(2,1)S(1)} %bitcast.345), channel_id=1, source_target_pairs={{0,4},{4,0},{8,12},{12,8},{16,20},{20,16},{24,28},{28,24},{1,5},{5... | collective-permute-start | bytes 76040 | tf_op jit(solution)/shard_map/ppermute | solution.py:30
  116.2 5.8 %copy-start = (f32[1,18,66,192]{3,2,1,0:T(8,128)S(1)}, f32[1,18,66,192]{3,2,1,0:T(8,128)}, u32[]{:S(2)}) copy-start(f32[1,18,66,192]{3,2,1,0:T(8,128)} %get-tuple-element.261) | copy-start | bytes 2737156
  117.3 8.8 %collective-permute-start.7 = (bf16[1,1,66,192]{3,1,2,0:T(2,128)(2,1)S(1)}, bf16[1,1,66,192]{3,1,2,0:T(2,128)(2,1)S(1)}, u32[]{:S(2)}, u32[]{:S(2)}) collective-permute-start(bf16[1,1,66,192]{3,1,2,0:T(2,128)(2,1)S(1)} %copy.142), channel_id=1, source_target_pairs={{0,2},{1,3},{4,6},{5,7},{8,10},{9,11},{12,14},{13,15},{16,18},{17,... | collective-permute-start | bytes 76040 | tf_op jit(solution)/shard_map/ppermute | solution.py:19
  121.8 3.2 %collective-permute-start.10 = (bf16[1,66,192]{2,0,1:T(2,128)(2,1)S(1)}, bf16[1,66,192]{2,0,1:T(2,128)(2,1)S(1)}, u32[]{:S(2)}, u32[]{:S(2)}) collective-permute-start(bf16[1,66,192]{2,0,1:T(2,128)(2,1)S(1)} %collective-permute-done.9), channel_id=1, source_target_pairs={{0,8},{4,12},{8,0},{12,4},{16,24},{20,28},{24,16},{28,20},{1,9},{5... | collective-permute-start | bytes 76040 | tf_op jit(solution)/shard_map/ppermute | solution.py:30
  125.0 4.8 %collective-permute-start.11 = (bf16[1,66,192]{2,0,1:T(2,128)(2,1)S(1)}, bf16[1,66,192]{2,0,1:T(2,128)(2,1)S(1)}, u32[]{:S(2)}, u32[]{:S(2)}) collective-permute-start(bf16[1,66,192]{2,0,1:T(2,128)(2,1)S(1)} %collective-permute-done.10), channel_id=1, source_target_pairs={{0,16},{4,20},{8,24},{12,28},{16,0},{20,4},{24,8},{28,12},{1,17},{... | collective-permute-start | bytes 76040 | tf_op jit(solution)/shard_map/ppermute | solution.py:30
  133.1 3.1 %copy-start.3 = (bf16[1,1,16,4,16,192]{5,4,2,3,0,1:T(8,128)(2,1)S(1)}, bf16[1,1,16,4,16,192]{5,4,2,3,0,1:T(8,128)(2,1)}, u32[]{:S(2)}) copy-start(bf16[1,1,16,4,16,192]{5,4,2,3,0,1:T(8,128)(2,1)} %slice_bitcast_fusion) | copy-start | bytes 1179652
  133.1 4.3 %collective-permute-start.12 = (f32[1,16,1,192]{3,1,0,2:T(8,128)S(1)}, f32[1,16,1,192]{3,1,0,2:T(8,128)S(1)}, u32[]{:S(2)}, u32[]{:S(2)}) collective-permute-start(f32[1,16,1,192]{3,1,0,2:T(8,128)S(1)} %get-tuple-element.327), channel_id=1, source_target_pairs={{0,4},{4,8},{8,12},{12,16},{16,20},{20,24},{24,28},{28,0},{1,5},{5... | collective-permute-start | bytes 36872 | tf_op jit(solution)/shard_map/ppermute | solution.py:19
  137.1 3.2 %collective-permute-start.13 = (f32[1,16,1,192]{3,1,0,2:T(8,128)S(1)}, f32[1,16,1,192]{3,1,0,2:T(8,128)S(1)}, u32[]{:S(2)}, u32[]{:S(2)}) collective-permute-start(f32[1,16,1,192]{3,1,0,2:T(8,128)S(1)} %get-tuple-element.326), channel_id=1, source_target_pairs={{4,0},{8,4},{12,8},{16,12},{20,16},{24,20},{28,24},{0,28},{5,1},{9... | collective-permute-start | bytes 36872 | tf_op jit(solution)/shard_map/ppermute | solution.py:22
Sparse Core Ops, SparseCore 0:
  137.1 131.7 all-reduce.2
where the time goes:
time: 281 us; the launch traced here: 279 us
  waiting for transfers between devices  137 us (49%)
  local copies, waits for them, and re-layouts  60.2 us (21%)
  matrix products  23.5 us (8%)
  starting transfers between devices  22.3 us (8%)
  other arithmetic  14.5 us (5%)
  between operations  14.5 us (5%)
  loops' own time  6.1 us (2%)
    psum x1, waiting for transfers between devices, body(): summed = lax.psum(partial_kernel, ('lon', 'lat', 'dp'))  127 us
    scatter-add x7, local copies, waits for them, and re-layouts, body(): grad_windows = grad_windows.at[:, :, row_shift:row_shift + TS, col_shift:...  25.6 us
    ppermute x4, starting transfers between devices, with_halo(): lax.ppermute(lax.slice_in_dim(block, block.shape[dim] - width, None, axis...  12.8 us
    dot_general x9, matrix products, body(): jnp.einsum('sbyxd,cd->sbyxc', grad_pre, kernel[row_shift, col_shift], pre...  12.1 us
    dynamic_update_slice x3, local copies, waits for them, and re-layouts, place(): return lax.dynamic_update_slice(total, current + grad_windows[slot], spot)  10.2 us
    dot_general x9, matrix products, body(): jnp.einsum('sbyxc,sbyxd->cd', piece, grad_pre, preferred_element_type=jnp...  8.8 us
    ppermute x6, waiting for transfers between devices, from_partner(): return lax.ppermute(value, axis, pairs)  7.04 us
    ppermute x6, starting transfers between devices, from_partner(): return lax.ppermute(value, axis, pairs)  6.55 us
  transfers between devices with their start and end apart: 15, of which 6 were waited for; matrix products, arithmetic and copies ran while one was open for 9% of the time, Pallas kernels for 0%

commit v1 on v0

v1 whole, which is shorter than its diff:
```python
import functools
import math

import jax
import jax.numpy as jnp
from jax import lax
from jax.experimental import pallas as pl
from jax.experimental.pallas import tpu as pltpu
from jax.sharding import PartitionSpec as P

TS = 16
LANE = 128
SUB = 16
MESH = pl.DeviceIdType.MESH
F32 = jnp.float32
BF16 = jnp.bfloat16
NORTH, SOUTH = 0, 1


def iota(shape, axis):
    return lax.broadcasted_iota(jnp.int32, shape, axis)


def mm(a, b, dims=((1,), (0,))):
    return lax.dot_general(a, b, (dims, ((), ())), preferred_element_type=F32)


def onehot(cond):
    return jnp.where(cond, 1.0, 0.0).astype(BF16)


def kernel_body(
    geo,
    states, cotangent, weights, land, tiles,
    out, sgrad, wgrad,
    own, colsend, colrecv, halo, wide_x, wide_g, lag_g, k_fwd, k_bwd, k_north,
    wf, wb, r1, a1, b1, r2, a2, b2, r3, ag,
    hs_send, hs_recv, s1, q1, s2, q2, s3, q3, s4, q4, s5, q5, s6, q6,
):
    n_lon, n_lat, n_dp, scale = geo
    _, rows, cols, ch = states.shape
    cells = rows * cols
    wide = 2 * LANE
    lon, lat, dp = lax.axis_index("lon"), lax.axis_index("lat"), lax.axis_index("dp")
    core, z = lax.rem(lon, 2), lon // 2
    nz, npl = n_lon // 2, n_lat * n_dp
    plane = lat * n_dp + dp
    left = {"lon": lax.rem(lon + n_lon - 1, n_lon)}
    right = {"lon": lax.rem(lon + 1, n_lon)}
    top = lat == n_lat - 1
    mirror = {"lon": n_lon - 1 - lon}
    upward = {
        "lon": jnp.where(top, n_lon - 1 - lon, lon),
        "lat": jnp.where(top, lat, lat + 1),
    }
    up_slot = jnp.where(top, NORTH, SOUTH)
    downward = {"lat": jnp.maximum(lat - 1, 0)}
    pair = {"lon": lon + 1 - 2 * core}

    def plane_peer(d):
        index = lax.rem(plane + d, npl)
        return index, {"lat": index // n_dp, "dp": lax.rem(index, n_dp)}

    def z_peer(d):
        index = lax.rem(z + d, nz)
        return index, {"lon": index * 2 + core}

    def remote(src, dst, send, recv, where):
        return pltpu.make_async_remote_copy(
            src_ref=src, dst_ref=dst, send_sem=send, recv_sem=recv,
            device_id=where, device_id_type=MESH,
        )

    barrier = pltpu.get_barrier_semaphore()

    def greet(where):
        pl.semaphore_signal(barrier, inc=1, device_id=where, device_id_type=MESH)

    greet(left)
    greet(right)
    for d in range(1, npl):
        greet(plane_peer(d)[1])
    for d in range(1, nz):
        greet(z_peer(d)[1])

    @pl.when(top)
    def _():
        greet(mirror)

    tile_cols = cols // TS
    number = iota((rows, cols), 0) // TS * tile_cols + iota((rows, cols), 1) // TS
    hit = number == tiles[0, 0, 0]
    for slot in range(1, tiles.shape[2]):
        hit = hit | (number == tiles[0, 0, slot])
    keep_plane = jnp.where(hit, land[...], 0).astype(F32).astype(BF16)
    cell = iota((cells, rows), 0) - cols * iota((cells, rows), 1)
    by_row = mm(onehot((cell >= 0) & (cell < cols)), keep_plane)
    pos = lax.rem(iota((cells, cols), 0), cols)
    by_cell = jnp.where(pos == iota((cells, cols), 1), by_row, 0.0).astype(BF16)
    keep = mm(by_cell, jnp.ones((cols, ch), BF16))
    column = lax.rem(iota((cells, ch), 0), cols)
    at_first, at_last = column == 0, column == cols - 1
    first_of = onehot(cell == 0)
    last_of = onehot(cell == cols - 1)
    pick = iota((2 * rows, cells), 1) - jnp.where(
        iota((2 * rows, cells), 0) < rows,
        cols * iota((2 * rows, cells), 0),
        cols * (iota((2 * rows, cells), 0) - rows) + cols - 1,
    )
    pick = onehot(pick == 0)

    masked = jnp.where(keep > 0, states[...].reshape(cells, ch).astype(F32), 0.0)
    own[0] = masked.astype(BF16)
    colsend[0] = mm(pick, own[0]).astype(BF16)

    k_fwd[...] = jnp.zeros_like(k_fwd)
    k_bwd[...] = jnp.zeros_like(k_bwd)
    k_north[...] = jnp.zeros_like(k_north)
    wide_x[...] = jnp.zeros_like(wide_x)
    wide_g[...] = jnp.zeros_like(wide_g)
    lag_g[...] = jnp.zeros_like(lag_g)
    for r in range(3):
        for c in range(3):
            k_fwd[r, c * wide : c * wide + ch, :] = weights[r, c]
            k_bwd[r, :, c * wide : c * wide + ch] = weights[r, c]

    @pl.when(top)
    def _():
        for c in range(3):
            k_north[:, c * wide : c * wide + ch] = weights[2, 2 - c]

    @pl.when(jnp.logical_not(top))
    def _():
        for c in range(3):
            k_north[:, c * wide : c * wide + ch] = weights[0, c]

    @pl.when(lat == 0)
    def _():
        for which in range(2):
            halo[which, SOUTH] = jnp.zeros_like(halo[which, SOUTH])

    pl.semaphore_wait(barrier, 2 + (npl - 1) + (nz - 1) + jnp.where(top, 1, 0))

    def first_copies(w):
        send, recv = hs_send.at[w], hs_recv.at[w]
        to_left = remote(
            colsend.at[w, pl.ds(0, rows)], colrecv.at[w, pl.ds(rows, rows)],
            send.at[0], recv.at[0], left)
        to_right = remote(
            colsend.at[w, pl.ds(rows, rows)], colrecv.at[w, pl.ds(0, rows)],
            send.at[1], recv.at[1], right)
        up = remote(
            own.at[w, pl.ds(cells - cols, cols)], halo.at[w, up_slot, pl.ds(0, cols)],
            send.at[2], recv.at[2 + up_slot], upward)
        down = remote(
            own.at[w, pl.ds(0, cols)], halo.at[w, NORTH, pl.ds(0, cols)],
            send.at[3], recv.at[2 + NORTH], downward)
        return to_left, to_right, up, down

    def corner_copies(w):
        send, recv = hs_send.at[w], hs_recv.at[w]
        up = remote(
            colrecv.at[w], halo.at[w, up_slot, pl.ds(cols, 2 * rows)],
            send.at[4], recv.at[4 + up_slot], upward)
        down = remote(
            colrecv.at[w], halo.at[w, NORTH, pl.ds(cols, 2 * rows)],
            send.at[5], recv.at[4 + NORTH], downward)
        return up, down

    def start_first(w):
        to_left, to_right, up, down = first_copies(w)
        to_left.start()
        to_right.start()
        up.start()

        @pl.when(lat > 0)
        def _():
            down.start()

    def pass_corners(w):
        to_left, to_right, _, _ = first_copies(w)
        to_left.wait_recv()
        to_right.wait_recv()
        up, down = corner_copies(w)
        up.start()

        @pl.when(lat > 0)
        def _():
            down.start()

    def finish_halo(w):
        send, recv = hs_send.at[w], hs_recv.at[w]

        def arrived(slot):
            remote(own.at[w, pl.ds(0, cols)], halo.at[w, slot, pl.ds(0, cols)],
                   send.at[3], recv.at[2 + slot], downward).wait_recv()
            remote(colrecv.at[w], halo.at[w, slot, pl.ds(cols, 2 * rows)],
                   send.at[5], recv.at[4 + slot], downward).wait_recv()

        arrived(NORTH)

        @pl.when(lat > 0)
        def _():
            arrived(SOUTH)

    def finish_sends(w):
        to_left, to_right, up, down = first_copies(w)
        up2, down2 = corner_copies(w)
        for copy in (to_left, to_right, up, up2):
            copy.wait_send()

        @pl.when(lat > 0)
        def _():
            down.wait_send()
            down2.wait_send()

    def spread(w, ref, values, order):
        lane = [b * wide for b in order]
        body = pl.ds(cols, cells)
        ref[body, lane[1] : lane[1] + ch] = own[w]
        low = mm(first_of, colrecv[w, :rows])
        ref[body, lane[0] : lane[0] + ch] = jnp.where(
            at_first, low, pltpu.roll(values, 1, 0)
        ).astype(BF16)
        high = mm(last_of, colrecv[w, rows:])
        ref[body, lane[2] : lane[2] + ch] = jnp.where(
            at_last, high, pltpu.roll(values, cells - 1, 0)
        ).astype(BF16)

    def spread_halo(w, ref, order):
        shape = (3 * cols, cols + 2 * rows)
        p, s = iota(shape, 0), iota(shape, 1)
        block = jnp.where(p >= cols, 1, 0) + jnp.where(p >= 2 * cols, 1, 0)
        east = p - cols * block + block - 1
        flip = jnp.where(top, 1, 0)
        for slot, at in ((NORTH, cells + cols), (SOUTH, 0)):
            if slot == NORTH:
                e = east + flip * (cols - 1 - 2 * east)
                edge = flip * (rows - 1)
            else:
                e, edge = east, rows - 1
            source = jnp.where(
                e < 0, cols + edge, jnp.where(e >= cols, cols + rows + edge, e))
            got = mm(onehot(s == source), halo[w, slot]).astype(BF16)
            for b in range(3):
                ref[at : at + cols, order[b] * wide : order[b] * wide + ch] = got[
                    b * cols : (b + 1) * cols
                ]

    start_first(0)
    pass_corners(0)
    spread(0, wide_x, masked, (0, 1, 2))
    finish_halo(0)
    spread_halo(0, wide_x, (0, 1, 2))

    pre = mm(wide_x[0:cells, :], k_fwd[0])
    pre = pre + mm(wide_x[cols : cols + cells, :], k_fwd[1])
    pre = pre + mm(wide_x[2 * cols : 2 * cols + cells, :], k_fwd[2])
    sig = 1.0 / (1.0 + jnp.exp(-pre))
    out[...] = (keep * pre * sig).astype(BF16).reshape(out.shape)
    slope = sig * (1.0 + pre * (1.0 - sig))
    grad = (keep * cotangent[...].reshape(cells, ch).astype(F32) * slope).astype(BF16)
    own[1] = grad
    for r in range(3):
        lag_g[r * cols : r * cols + cells, r * wide : r * wide + ch] = grad
    colsend[1] = mm(pick, own[1]).astype(BF16)
    start_first(1)

    full = mm(wide_x[...], lag_g[...], ((0,), (0,)))
    units = ch // SUB
    total = wf.shape[0]

    def put(slab, value):
        value = value.reshape(units, SUB, LANE)
        wf[slab * units : (slab + 1) * units] = value
        wb[slab * units : (slab + 1) * units] = value.astype(BF16)

    tails = []
    for c in range(3):
        band = full[c * wide : c * wide + ch]
        for r in range(3):
            put(3 * c + r, band[:, r * wide : r * wide + LANE])
        rest = [band[:, r * wide + LANE : (r + 1) * wide] for r in range(3)]
        put(9 + c, rest[0] + pltpu.roll(rest[1], LANE // 2, 1))
        tails.append(rest[2])
    put(12, tails[0] + pltpu.roll(tails[1], LANE // 2, 1))
    put(13, tails[2])
    if total > 14 * units:
        wf[14 * units :] = jnp.zeros_like(wf[14 * units :])
        wb[14 * units :] = jnp.zeros_like(wb[14 * units :])

    half = total // 2
    per = half // npl
    chunk = -(-per // nz)
    pair_copy = remote(
        wb.at[pl.ds((1 - core) * half, half)], r1, s1.at[0], q1.at[0], pair)
    pair_copy.start()
    pass_corners(1)
    spread(1, wide_g, grad.astype(F32), (2, 1, 0))
    pair_copy.wait()
    first = wf[pl.ds(core * half, half)] + r1[...].astype(F32)
    a1[...] = first.reshape(a1.shape)
    b1[...] = first.reshape(a1.shape).astype(BF16)
    plane_copies = []
    for d in range(1, npl):
        index, where = plane_peer(d)
        copy = remote(b1.at[index], r2.at[d - 1], s2.at[d - 1], q2.at[d - 1], where)
        copy.start()
        plane_copies.append(copy)

    finish_halo(1)
    spread_halo(1, wide_g, (2, 1, 0))
    nt = ((1,), (1,))
    back = mm(wide_g[cols : cols + cells, :], k_bwd[1], nt)
    back = back + mm(wide_g[0:cells, :], k_bwd[2], nt)
    inner = mm(wide_g[2 * cols : cols + cells, :], k_bwd[0], nt)
    edge = mm(wide_g[cols + cells : 2 * cols + cells, :], k_north[...], nt)
    back = back + jnp.concatenate([inner, edge], axis=0)
    sgrad[...] = jnp.where(keep > 0, back, 0.0).astype(BF16).reshape(sgrad.shape)

    for copy in plane_copies:
        copy.wait()
    second = a1[plane]
    for d in range(npl - 1):
        second = second + r2[d].astype(F32)
    a2[0:per] = second
    b2[0:per] = second.astype(BF16)
    if nz * chunk > per:
        a2[per:] = jnp.zeros_like(a2[per:])
        b2[per:] = jnp.zeros_like(b2[per:])
    z_copies = []
    for d in range(1, nz):
        index, where = z_peer(d)
        copy = remote(
            b2.at[pl.ds(index * chunk, chunk)], r3.at[d - 1],
            s3.at[d - 1], q3.at[d - 1], where)
        copy.start()
        z_copies.append(copy)
    for copy in z_copies:
        copy.wait()
    third = a2[pl.ds(z * chunk, chunk)]
    for d in range(nz - 1):
        third = third + r3[d].astype(F32)
    mine = pl.ds(z * chunk, chunk)
    ag[core, plane, mine] = (third * scale).astype(BF16)

    z_back = []
    for d in range(1, nz):
        _, where = z_peer(d)
        here = ag.at[core, plane, mine]
        copy = remote(here, here, s4.at[d - 1], q4.at[d - 1], where)
        copy.start()
        z_back.append(copy)
    for d in range(1, nz):
        source = lax.rem(z + nz - d, nz)
        there = ag.at[core, plane, pl.ds(source * chunk, chunk)]
        remote(there, there, s4.at[d - 1], q4.at[d - 1], pair).wait_recv()
    whole = pl.ds(0, per)
    here = ag.at[core, plane, whole]
    plane_back = []
    for d in range(1, npl):
        _, where = plane_peer(d)
        copy = remote(here, here, s5.at[d - 1], q5.at[d - 1], where)
        copy.start()
        plane_back.append(copy)
    core_back = [remote(here, here, s6.at[0], q6.at[0], pair)]
    core_back[0].start()
    for d in range(1, npl):
        source = lax.rem(plane + npl - d, npl)
        there = ag.at[core, source, whole]
        remote(there, there, s5.at[d - 1], q5.at[d - 1], pair).wait_recv()
        copy = remote(there, there, s6.at[d], q6.at[d], pair)
        copy.start()
        core_back.append(copy)
    for d in range(npl):
        source = lax.rem(plane + npl - d, npl)
        there = ag.at[1 - core, source, whole]
        remote(there, there, s6.at[d], q6.at[d], pair).wait_recv()

    def slab(s):
        found = []
        for t in range(s * units, (s + 1) * units):
            found.append(ag[t // half, t % half // per, t % per])
        return jnp.concatenate(found, axis=0).astype(F32)

    hl = LANE // 2
    for c in range(3):
        for r in range(3):
            wgrad[r, c, :, 0:LANE] = slab(3 * c + r)
        rest = slab(9 + c)
        wgrad[0, c, :, LANE:ch] = rest[:, 0:hl]
        wgrad[1, c, :, LANE:ch] = pltpu.roll(rest, hl, 1)[:, 0:hl]
    rest = slab(12)
    wgrad[2, 0, :, LANE:ch] = rest[:, 0:hl]
    wgrad[2, 1, :, LANE:ch] = pltpu.roll(rest, hl, 1)[:, 0:hl]
    wgrad[2, 2, :, LANE:ch] = slab(13)[:, 0:hl]

    finish_sends(0)
    finish_sends(1)
    for copy in z_back + plane_back + core_back:
        copy.wait_send()


def body(states, cotangent, weights, land_mask, ocean_tiles):
    n_lon, n_lat, n_dp = (lax.axis_size(a) for a in ("lon", "lat", "dp"))
    batch, rows, cols, ch = states.shape
    assert batch == 1 and ch == 192 and n_lon % 2 == 0
    cells = rows * cols
    count = batch * n_dp * rows * n_lat * cols * n_lon
    wide = 2 * LANE
    nz, npl = n_lon // 2, n_lat * n_dp
    groups = 2 * npl
    total = -(-14 * (ch // SUB) // groups) * groups
    half = total // 2
    per = half // npl
    chunk = -(-per // nz)
    tile = (SUB, LANE)
    vmem = pltpu.VMEM
    dma = pltpu.SemaphoreType.DMA
    scratch = [
        vmem((2, cells, ch), BF16),
        vmem((2, 2 * rows, ch), BF16),
        vmem((2, 2 * rows, ch), BF16),
        vmem((2, 2, cols + 2 * rows, ch), BF16),
        vmem((cells + 2 * cols, 3 * wide), BF16),
        vmem((cells + 2 * cols, 3 * wide), BF16),
        vmem((cells + 2 * cols, 3 * wide), BF16),
        vmem((3, 3 * wide, ch), BF16),
        vmem((3, ch, 3 * wide), BF16),
        vmem((ch, 3 * wide), BF16),
        vmem((total,) + tile, F32),
        vmem((total,) + tile, BF16),
        vmem((half,) + tile, BF16),
        vmem((npl, per) + tile, F32),
        vmem((npl, per) + tile, BF16),
        vmem((npl - 1, per) + tile, BF16),
        vmem((nz * chunk,) + tile, F32),
        vmem((nz * chunk,) + tile, BF16),
        vmem((nz - 1, chunk) + tile, BF16),
        vmem((2, npl, nz * chunk) + tile, BF16),
        dma((2, 6)), dma((2, 6)),
        dma((1,)), dma((1,)),
        dma((npl - 1,)), dma((npl - 1,)),
        dma((nz - 1,)), dma((nz - 1,)),
        dma((nz - 1,)), dma((nz - 1,)),
        dma((npl - 1,)), dma((npl - 1,)),
        dma((npl,)), dma((npl,)),
    ]
    in_vmem = pl.BlockSpec(memory_space=pltpu.VMEM)
    geo = (n_lon, n_lat, n_dp, 1.0 / math.sqrt(count))
    return pl.pallas_call(
        functools.partial(kernel_body, geo),
        out_shape=(
            jax.ShapeDtypeStruct(states.shape, BF16),
            jax.ShapeDtypeStruct(states.shape, BF16),
            jax.ShapeDtypeStruct(weights.shape, F32),
        ),
        in_specs=[in_vmem] * 4 + [pl.BlockSpec(memory_space=pltpu.SMEM)],
        out_specs=(in_vmem,) * 3,
        scratch_shapes=scratch,
        compiler_params=pltpu.CompilerParams(
            collective_id=0, has_side_effects=True, vmem_limit_bytes=48 * 2**20
        ),
        cost_estimate=pl.CostEstimate(
            flops=54 * cells * ch * ch, bytes_accessed=5_000_000, transcendentals=cells * ch
        ),
    )(states, cotangent, weights, land_mask, ocean_tiles)


def solution(mesh):
    in_specs = (
        P("dp", "lat", "lon", None),
        P("dp", "lat", "lon", None),
        P(),
        P("lat", "lon"),
        P("lat", "lon", None),
    )
    out_specs = (P("dp", "lat", "lon", None), P("dp", "lat", "lon", None), P())
    return jax.shard_map(body, mesh=mesh, in_specs=in_specs, out_specs=out_specs, check_vma=False)
```

time: 281 us -> 48 us (0.17)
  waiting for transfers between devices: 137 us -> 0 us
  local copies, waits for them, and re-layouts: 60.2 us -> 7.39 us
  Pallas kernels: 0 us -> 39.7 us
  matrix products: 23.5 us -> 0 us
  starting transfers between devices: 22.3 us -> 0 us
  other arithmetic: 14.5 us -> 0 us
  between operations: 14.5 us -> 0.65 us
  loops' own time: 6.1 us -> 0 us
    psum x1 -> x0, waiting for transfers between devices: 127 us -> none  [body(): summed = lax.psum(partial_kernel, ('lon', 'lat', 'dp'))]
    pallas_call x0 -> x1, Pallas kernels: none -> 39.7 us  [body(): pl.pallas_call(functools.partial(kernel_body, geo), out_shape=(jax.ShapeD...]
    scatter-add x9 -> x0, local copies, waits for them, and re-layouts: 31.3 us -> none  [the longest x7 25.6 us: body(): grad_windows = grad_windows.at[:, :, row_shift:row_shift + TS, col_shift:...]
    dot_general x27 -> x0, matrix products: 23.5 us -> none  [the longest x9 12.1 us: body(): jnp.einsum('sbyxd,cd->sbyxc', grad_pre, kernel[row_shift, col_shift], pre...]
    ppermute x14 -> x0, starting transfers between devices: 22.3 us -> none  [the longest x4 12.8 us: with_halo(): lax.ppermute(lax.slice_in_dim(block, block.shape[dim] - width, None, axis...]
    dynamic_update_slice x3 -> x0, local copies, waits for them, and re-layouts: 10.2 us -> none  [place(): return lax.dynamic_update_slice(total, current + grad_windows[slot], spot)]
    ppermute x14 -> x0, waiting for transfers between devices: 9.93 us -> none  [the longest x6 7.04 us: from_partner(): return lax.ppermute(value, axis, pairs)]
    another operation x2 -> x0, loops' own time: 6.1 us -> none  [the longest x1 6.08 us: body(): lax.fori_loop(0, capacity, place, jnp.zeros((batch_size, row_count + 2, c...]
  transfers between devices with their start and end apart: 15 -> 0, of which waited for: 6 -> 0; matrix products, arithmetic and copies ran while one was open for 9% -> 0% of each run, Pallas kernels for 0% -> 0%
where the time goes in v1:
time: 48 us; the launch traced here: 47.7 us
  Pallas kernels  39.7 us (83%)
  local copies, waits for them, and re-layouts  7.39 us (15%)
  between operations  0.65 us (1%)
    pallas_call x1, Pallas kernels, body(): pl.pallas_call(functools.partial(kernel_body, geo), out_shape=(jax.ShapeD...  39.7 us
    unnamed x13, local copies, waits for them, and re-layouts  7.39 us

profile of v1, /device:TPU:1, one launch (start us, length us, event | category | flops | bytes accessed | tf_op | source)
XLA Modules:
  0.0 47.7 jit_solution(14165392321252076514)
XLA Ops:
  0.6 0.0 copy-start
  0.6 1.2 %copy-done = bf16[3,3,192,192]{3,2,1,0:T(8,128)(2,1)S(1)} copy-done((bf16[3,3,192,192]{3,2,1,0:T(8,128)(2,1)S(1)}, bf16[3,3,192,192]{3,2,1,0:T(8,128)(2,1)}, u32[]{:S(2)}) %copy-start) | copy-done | bytes 663576
  1.8 0.0 copy-start.1
  1.8 1.0 %copy-done.1 = bf16[1,16,64,192]{3,2,1,0:T(8,128)(2,1)S(1)} copy-done((bf16[1,16,64,192]{3,2,1,0:T(8,128)(2,1)S(1)}, bf16[1,16,64,192]{3,2,1,0:T(8,128)(2,1)}, u32[]{:S(2)}) %copy-start.1) | copy-done | bytes 393240
  2.8 0.0 copy-start.2
  2.8 1.0 %copy-done.2 = bf16[1,16,64,192]{3,2,1,0:T(8,128)(2,1)S(1)} copy-done((bf16[1,16,64,192]{3,2,1,0:T(8,128)(2,1)S(1)}, bf16[1,16,64,192]{3,2,1,0:T(8,128)(2,1)}, u32[]{:S(2)}) %copy-start.2) | copy-done | bytes 393240
  3.9 0.0 copy-start.3
  3.9 0.7 %copy-done.3 = s32[16,64]{1,0:T(8,128)S(1)} copy-done((s32[16,64]{1,0:T(8,128)S(1)}, s32[16,64]{1,0:T(8,128)}, u32[]{:S(2)}) %copy-start.3) | copy-done | bytes 4120
  4.6 0.0 copy-start.4
  4.6 0.7 %copy-done.4 = s32[1,1,3]{2,1,0:T(1,128)S(1)} copy-done((s32[1,1,3]{2,1,0:T(1,128)S(1)}, s32[1,1,3]{2,1,0:T(1,128)}, u32[]{:S(2)}) %copy-start.4) | copy-done | bytes 36
  5.2 39.7 %shard_map.76 = (bf16[1,16,64,192]{3,2,1,0:T(8,128)(2,1)S(1)}, bf16[1,16,64,192]{3,2,1,0:T(8,128)(2,1)S(1)}, f32[3,3,192,192]{3,2,1,0:T(8,128)S(1)}) custom-call(bf16[1,16,64,192]{3,2,1,0:T(8,128)(2,1)S(1)} %copy-done.1, bf16[1,16,64,192]{3,2,1,0:T(8,128)(2,1)S(1)} %copy-done.2, bf16[3,3,192,192]{3,2,1,0:T(8,128)(2,1)S(1)} %copy-done, ...), custom_call_target="tpu_custom_call" | custom-call | flops 2038431744 | bytes 5000000 | tf_op jit(solution)/shard_map/pallas_call | solution.py:451
  44.9 0.8 %copy.11 = bf16[1,16,64,192]{3,2,1,0:T(8,128)(2,1)} copy(bf16[1,16,64,192]{3,2,1,0:T(8,128)(2,1)S(1)} %get-tuple-element.6) | data formatting | bytes 786432
  45.7 0.8 %copy.12 = bf16[1,16,64,192]{3,2,1,0:T(8,128)(2,1)} copy(bf16[1,16,64,192]{3,2,1,0:T(8,128)(2,1)S(1)} %get-tuple-element.7) | data formatting | bytes 786432
  46.5 1.2 %copy.13 = f32[3,3,192,192]{3,2,1,0:T(8,128)} copy(f32[3,3,192,192]{3,2,1,0:T(8,128)S(1)} %get-tuple-element.8) | data formatting | bytes 2654208
Async XLA Ops:
  0.6 1.2 %copy-start = (bf16[3,3,192,192]{3,2,1,0:T(8,128)(2,1)S(1)}, bf16[3,3,192,192]{3,2,1,0:T(8,128)(2,1)}, u32[]{:S(2)}) copy-start(bf16[3,3,192,192]{3,2,1,0:T(8,128)(2,1)} %weights.1) | copy-start | bytes 1990660
  1.8 1.0 %copy-start.1 = (bf16[1,16,64,192]{3,2,1,0:T(8,128)(2,1)S(1)}, bf16[1,16,64,192]{3,2,1,0:T(8,128)(2,1)}, u32[]{:S(2)}) copy-start(bf16[1,16,64,192]{3,2,1,0:T(8,128)(2,1)} %states.1) | copy-start | bytes 1179652
  2.8 1.0 %copy-start.2 = (bf16[1,16,64,192]{3,2,1,0:T(8,128)(2,1)S(1)}, bf16[1,16,64,192]{3,2,1,0:T(8,128)(2,1)}, u32[]{:S(2)}) copy-start(bf16[1,16,64,192]{3,2,1,0:T(8,128)(2,1)} %cotangent.1) | copy-start | bytes 1179652
  3.9 0.7 %copy-start.3 = (s32[16,64]{1,0:T(8,128)S(1)}, s32[16,64]{1,0:T(8,128)}, u32[]{:S(2)}) copy-start(s32[16,64]{1,0:T(8,128)} %land.1) | copy-start | bytes 12292
  4.6 0.7 %copy-start.4 = (s32[1,1,3]{2,1,0:T(1,128)S(1)}, s32[1,1,3]{2,1,0:T(1,128)}, u32[]{:S(2)}) copy-start(s32[1,1,3]{2,1,0:T(1,128)} %tiles.1) | copy-start | bytes 40

commit v2 on v1

v2 whole, which is shorter than its diff:
```python
import functools
import math

import jax
import jax.numpy as jnp
from jax import lax
from jax.experimental import pallas as pl
from jax.experimental.pallas import tpu as pltpu
from jax.sharding import PartitionSpec as P

TS = 16
LANE = 128
SUB = 16
MESH = pl.DeviceIdType.MESH
F32 = jnp.float32
BF16 = jnp.bfloat16
NORTH, SOUTH = 0, 1


def iota(shape, axis):
    return lax.broadcasted_iota(jnp.int32, shape, axis)


def mm(a, b, dims=((1,), (0,))):
    return lax.dot_general(a, b, (dims, ((), ())), preferred_element_type=F32)


def onehot(cond):
    return jnp.where(cond, 1.0, 0.0).astype(BF16)


def kernel_body(
    geo,
    states_hbm, cotangent_hbm, weights_hbm, land_hbm, tiles,
    out_hbm, sgrad_hbm, wgrad_hbm,
    out, sgrad, wgrad, states, cotangent, weights, land, in_sem, out_sem,
    own, colsend, colrecv, halo, wide_x, wide_g, lag_g, k_fwd, k_bwd, k_north,
    x_turned, parts, hs_send, hs_recv,
):
    n_lon, n_lat, n_dp, scale = geo
    _, rows, cols, ch = states.shape
    cells = rows * cols
    wide = 2 * LANE
    lon, lat, dp = lax.axis_index("lon"), lax.axis_index("lat"), lax.axis_index("dp")
    core, z = lax.rem(lon, 2), lon // 2
    nz, npl = n_lon // 2, n_lat * n_dp
    plane = lat * n_dp + dp
    left = {"lon": lax.rem(lon + n_lon - 1, n_lon)}
    right = {"lon": lax.rem(lon + 1, n_lon)}
    top = lat == n_lat - 1
    mirror = {"lon": n_lon - 1 - lon}
    upward = {
        "lon": jnp.where(top, n_lon - 1 - lon, lon),
        "lat": jnp.where(top, lat, lat + 1),
    }
    up_slot = jnp.where(top, NORTH, SOUTH)
    downward = {"lat": jnp.maximum(lat - 1, 0)}
    pair = {"lon": lon + 1 - 2 * core}

    def plane_peer(d):
        index = lax.rem(plane + d, npl)
        return index, {"lat": index // n_dp, "dp": lax.rem(index, n_dp)}

    def z_peer(d):
        index = lax.rem(z + d, nz)
        return index, {"lon": index * 2 + core}

    def remote(src, dst, send, recv, where):
        return pltpu.make_async_remote_copy(
            src_ref=src, dst_ref=dst, send_sem=send, recv_sem=recv,
            device_id=where, device_id_type=MESH,
        )

    fetch = []
    for i, (src, dst) in enumerate((
        (land_hbm, land), (states_hbm, states), (weights_hbm, weights),
        (cotangent_hbm, cotangent),
    )):
        copy = pltpu.make_async_copy(src, dst, in_sem.at[i])
        copy.start()
        fetch.append(copy)
    stores = []

    def store(src, dst):
        copy = pltpu.make_async_copy(src, dst, out_sem.at[len(stores)])
        copy.start()
        stores.append(copy)

    barrier = pltpu.get_barrier_semaphore()

    def greet(where):
        pl.semaphore_signal(barrier, inc=1, device_id=where, device_id_type=MESH)

    greet(left)
    greet(right)
    for d in range(1, npl):
        greet(plane_peer(d)[1])
    for d in range(1, nz):
        greet(z_peer(d)[1])

    @pl.when(top)
    def _():
        greet(mirror)

    tile_cols = cols // TS
    number = iota((rows, cols), 0) // TS * tile_cols + iota((rows, cols), 1) // TS
    hit = number == tiles[0, 0, 0]
    for slot in range(1, tiles.shape[2]):
        hit = hit | (number == tiles[0, 0, slot])
    fetch[0].wait()
    keep_plane = jnp.where(hit, land[...], 0).astype(F32).astype(BF16)
    cell = iota((cells, rows), 0) - cols * iota((cells, rows), 1)
    by_row = mm(onehot((cell >= 0) & (cell < cols)), keep_plane)
    pos = iota((cells, cols), 0) & (cols - 1)
    by_cell = jnp.where(pos == iota((cells, cols), 1), by_row, 0.0).astype(BF16)
    keep = mm(by_cell, jnp.ones((cols, ch), BF16))
    column = iota((cells, ch), 0) & (cols - 1)
    at_first, at_last = column == 0, column == cols - 1
    first_of = onehot(cell == 0)
    last_of = onehot(cell == cols - 1)
    pick = iota((2 * rows, cells), 1) - jnp.where(
        iota((2 * rows, cells), 0) < rows,
        cols * iota((2 * rows, cells), 0),
        cols * (iota((2 * rows, cells), 0) - rows) + cols - 1,
    )
    pick = onehot(pick == 0)

    fetch[1].wait()
    masked = jnp.where(keep > 0, states[...].reshape(cells, ch).astype(F32), 0.0)
    own[0] = masked.astype(BF16)
    colsend[0] = mm(pick, own[0]).astype(BF16)

    @pl.when(lat == 0)
    def _():
        for which in range(2):
            halo[which, SOUTH] = jnp.zeros_like(halo[which, SOUTH])

    pl.semaphore_wait(barrier, 2 + (npl - 1) + (nz - 1) + jnp.where(top, 1, 0))

    def first_copies(w):
        send, recv = hs_send.at[w], hs_recv.at[w]
        to_left = remote(
            colsend.at[w, pl.ds(0, rows)], colrecv.at[w, pl.ds(rows, rows)],
            send.at[0], recv.at[0], left)
        to_right = remote(
            colsend.at[w, pl.ds(rows, rows)], colrecv.at[w, pl.ds(0, rows)],
            send.at[1], recv.at[1], right)
        up = remote(
            own.at[w, pl.ds(cells - cols, cols)], halo.at[w, up_slot, pl.ds(0, cols)],
            send.at[2], recv.at[2 + up_slot], upward)
        down = remote(
            own.at[w, pl.ds(0, cols)], halo.at[w, NORTH, pl.ds(0, cols)],
            send.at[3], recv.at[2 + NORTH], downward)
        return to_left, to_right, up, down

    def corner_copies(w):
        send, recv = hs_send.at[w], hs_recv.at[w]
        up = remote(
            colrecv.at[w], halo.at[w, up_slot, pl.ds(cols, 2 * rows)],
            send.at[4], recv.at[4 + up_slot], upward)
        down = remote(
            colrecv.at[w], halo.at[w, NORTH, pl.ds(cols, 2 * rows)],
            send.at[5], recv.at[4 + NORTH], downward)
        return up, down

    def start_first(w):
        to_left, to_right, up, down = first_copies(w)
        to_left.start()
        to_right.start()
        up.start()

        @pl.when(lat > 0)
        def _():
            down.start()

    def pass_corners(w):
        to_left, to_right, _, _ = first_copies(w)
        to_left.wait_recv()
        to_right.wait_recv()
        up, down = corner_copies(w)
        up.start()

        @pl.when(lat > 0)
        def _():
            down.start()

    def finish_halo(w):
        send, recv = hs_send.at[w], hs_recv.at[w]

        def arrived(slot):
            remote(own.at[w, pl.ds(0, cols)], halo.at[w, slot, pl.ds(0, cols)],
                   send.at[3], recv.at[2 + slot], downward).wait_recv()
            remote(colrecv.at[w], halo.at[w, slot, pl.ds(cols, 2 * rows)],
                   send.at[5], recv.at[4 + slot], downward).wait_recv()

        arrived(NORTH)

        @pl.when(lat > 0)
        def _():
            arrived(SOUTH)

    def finish_sends(w):
        to_left, to_right, up, down = first_copies(w)
        up2, down2 = corner_copies(w)
        for copy in (to_left, to_right, up, up2):
            copy.wait_send()

        @pl.when(lat > 0)
        def _():
            down.wait_send()
            down2.wait_send()

    def spread(w, ref, values, order):
        lane = [b * wide for b in order]
        body = pl.ds(cols, cells)
        ref[body, lane[1] : lane[1] + ch] = own[w]
        low = mm(first_of, colrecv[w, :rows])
        ref[body, lane[0] : lane[0] + ch] = jnp.where(
            at_first, low, pltpu.roll(values, 1, 0)
        ).astype(BF16)
        high = mm(last_of, colrecv[w, rows:])
        ref[body, lane[2] : lane[2] + ch] = jnp.where(
            at_last, high, pltpu.roll(values, cells - 1, 0)
        ).astype(BF16)

    def spread_halo(w, ref, order):
        shape = (3 * cols, cols + 2 * rows)
        p, s = iota(shape, 0), iota(shape, 1)
        block = jnp.where(p >= cols, 1, 0) + jnp.where(p >= 2 * cols, 1, 0)
        east = p - cols * block + block - 1
        flip = jnp.where(top, 1, 0)
        for slot, at in ((NORTH, cells + cols), (SOUTH, 0)):
            if slot == NORTH:
                e = east + flip * (cols - 1 - 2 * east)
                edge = flip * (rows - 1)
            else:
                e, edge = east, rows - 1
            source = jnp.where(
                e < 0, cols + edge, jnp.where(e >= cols, cols + rows + edge, e))
            got = mm(onehot(s == source), halo[w, slot]).astype(BF16)
            for b in range(3):
                ref[at : at + cols, order[b] * wide : order[b] * wide + ch] = got[
                    b * cols : (b + 1) * cols
                ]

    start_first(0)
    fetch[2].wait()
    k_north[...] = jnp.zeros_like(k_north)
    for c in range(3):
        gap = pl.ds(c * wide + LANE, LANE)
        for ref in (wide_x, wide_g, lag_g):
            ref[:, gap] = jnp.zeros((ref.shape[0], LANE), BF16)
        for lo, hi in ((0, c * cols), (c * cols + cells, cells + 2 * cols)):
            if hi > lo:
                lag_g[lo:hi, c * wide : (c + 1) * wide] = jnp.zeros((hi - lo, wide), BF16)
    for r in range(3):
        k_bwd[r] = jnp.zeros_like(k_bwd[r])
        k_fwd[r] = jnp.zeros_like(k_fwd[r])
    for r in range(3):
        for c in range(3):
            k_fwd[r, c * wide : c * wide + ch, :] = weights[r, c]
            k_bwd[r, :, c * wide : c * wide + ch] = weights[r, c]

    @pl.when(top)
    def _():
        for c in range(3):
            k_north[:, c * wide : c * wide + ch] = weights[2, 2 - c]

    @pl.when(jnp.logical_not(top))
    def _():
        for c in range(3):
            k_north[:, c * wide : c * wide + ch] = weights[0, c]

    pass_corners(0)
    spread(0, wide_x, masked, (0, 1, 2))
    pre = mm(wide_x[cols : cols + cells, :], k_fwd[1])
    low = mm(wide_x[cols:cells, :], k_fwd[0])
    high = mm(wide_x[2 * cols : cols + cells, :], k_fwd[2])
    finish_halo(0)
    spread_halo(0, wide_x, (0, 1, 2))
    low_edge = mm(wide_x[0:cols, :], k_fwd[0])
    high_edge = mm(wide_x[cells + cols :, :], k_fwd[2])
    pre = pre + jnp.concatenate([low_edge, low], axis=0)
    pre = pre + jnp.concatenate([high, high_edge], axis=0)
    fetch[3].wait()
    for c in range(3):
        x_turned[c] = wide_x[:, c * wide : (c + 1) * wide].T
    sig = 1.0 / (1.0 + jnp.exp(-pre))
    out[...] = (keep * pre * sig).astype(BF16).reshape(out.shape)
    store(out, out_hbm)
    slope = sig * (1.0 + pre * (1.0 - sig))
    grad = (keep * cotangent[...].reshape(cells, ch).astype(F32) * slope).astype(BF16)
    own[1] = grad
    for r in range(3):
        lag_g[r * cols : r * cols + cells, r * wide : r * wide + ch] = grad
    colsend[1] = mm(pick, own[1]).astype(BF16)
    start_first(1)

    units = ch // SUB
    hl = LANE // 2
    tails = {}

    def add_up(p):
        q = parts[p]
        full = mm(x_turned[p], lag_g[...])
        band = full[:ch]
        slabs = [band[:, r * wide : r * wide + LANE] for r in range(3)]
        rest = [band[:, r * wide + LANE : (r + 1) * wide] for r in range(3)]
        slabs.append(rest[0] + pltpu.roll(rest[1], hl, 1))
        tails[p] = rest[2]
        if p == 1:
            slabs.append(tails[0] + pltpu.roll(tails[1], hl, 1))
        if p == 2:
            slabs.append(tails[2])
        for at, value in enumerate(slabs):
            value = value.reshape(units, SUB, LANE)
            q["wf"][at * units : (at + 1) * units] = value
            q["wb"][at * units : (at + 1) * units] = value.astype(BF16)
        used = len(slabs) * units
        total = q["wf"].shape[0]
        if total > used:
            q["wf"][used:] = jnp.zeros_like(q["wf"][used:])
            q["wb"][used:] = jnp.zeros_like(q["wb"][used:])
        half = total // 2
        q["half"], q["per"] = half, half // npl
        q["chunk"] = q["r3"].shape[1]
        q["pair"] = remote(
            q["wb"].at[pl.ds((1 - core) * half, half)], q["r1"],
            q["s"].at[0, 0], q["q"].at[0, 0], pair)
        q["pair"].start()

    def over_plane(p):
        q = parts[p]
        half = q["half"]
        q["pair"].wait()
        first = q["wf"][pl.ds(core * half, half)] + q["r1"][...].astype(F32)
        q["a1"][...] = first.reshape(q["a1"].shape)
        q["b1"][...] = first.reshape(q["a1"].shape).astype(BF16)
        q["plane"] = []
        for d in range(1, npl):
            index, where = plane_peer(d)
            copy = remote(q["b1"].at[index], q["r2"].at[d - 1],
                          q["s"].at[1, d - 1], q["q"].at[1, d - 1], where)
            copy.start()
            q["plane"].append(copy)

    def over_z(p):
        q = parts[p]
        per, chunk = q["per"], q["chunk"]
        for copy in q["plane"]:
            copy.wait()
        second = q["a1"][plane]
        for d in range(npl - 1):
            second = second + q["r2"][d].astype(F32)
        q["a2"][0:per] = second
        q["b2"][0:per] = second.astype(BF16)
        if nz * chunk > per:
            q["a2"][per:] = jnp.zeros_like(q["a2"][per:])
            q["b2"][per:] = jnp.zeros_like(q["b2"][per:])
        q["z"] = []
        for d in range(1, nz):
            index, where = z_peer(d)
            copy = remote(q["b2"].at[pl.ds(index * chunk, chunk)], q["r3"].at[d - 1],
                          q["s"].at[2, d - 1], q["q"].at[2, d - 1], where)
            copy.start()
            q["z"].append(copy)

    def z_return(p):
        q = parts[p]
        chunk = q["chunk"]
        for copy in q["z"]:
            copy.wait()
        mine = pl.ds(z * chunk, chunk)
        third = q["a2"][mine]
        for d in range(nz - 1):
            third = third + q["r3"][d].astype(F32)
        here = q["ag"].at[core, plane, mine]
        q["ag"][core, plane, mine] = (third * scale).astype(BF16)
        q["sent"] = []
        for d in range(1, nz):
            copy = remote(here, here, q["s"].at[3, d - 1], q["q"].at[3, d - 1], z_peer(d)[1])
            copy.start()
            q["sent"].append(copy)

    def plane_return(p):
        q = parts[p]
        chunk, per = q["chunk"], q["per"]
        for d in range(1, nz):
            source = lax.rem(z + nz - d, nz)
            there = q["ag"].at[core, plane, pl.ds(source * chunk, chunk)]
            remote(there, there, q["s"].at[3, d - 1], q["q"].at[3, d - 1], pair).wait_recv()
        here = q["ag"].at[core, plane, pl.ds(0, per)]
        for d in range(1, npl):
            copy = remote(here, here, q["s"].at[4, d - 1], q["q"].at[4, d - 1], plane_peer(d)[1])
            copy.start()
            q["sent"].append(copy)
        copy = remote(here, here, q["s"].at[5, 0], q["q"].at[5, 0], pair)
        copy.start()
        q["sent"].append(copy)

    def core_return(p):
        q = parts[p]
        for d in range(1, npl):
            source = lax.rem(plane + npl - d, npl)
            there = q["ag"].at[core, source, pl.ds(0, q["per"])]
            remote(there, there, q["s"].at[4, d - 1], q["q"].at[4, d - 1], pair).wait_recv()
            copy = remote(there, there, q["s"].at[5, d], q["q"].at[5, d], pair)
            copy.start()
            q["sent"].append(copy)

    def hand_out(p):
        q = parts[p]
        half, per = q["half"], q["per"]
        for d in range(npl):
            source = lax.rem(plane + npl - d, npl)
            there = q["ag"].at[1 - core, source, pl.ds(0, per)]
            remote(there, there, q["s"].at[5, d], q["q"].at[5, d], pair).wait_recv()

        def slab(at):
            found = []
            for t in range(at * units, (at + 1) * units):
                found.append(q["ag"][t // half, t % half // per, t % per])
            return jnp.concatenate(found, axis=0).astype(F32)

        for r in range(3):
            wgrad[r, p, :, 0:LANE] = slab(r)
        rest = slab(3)
        wgrad[0, p, :, LANE:ch] = rest[:, 0:hl]
        wgrad[1, p, :, LANE:ch] = pltpu.roll(rest, hl, 1)[:, 0:hl]
        if p == 1:
            rest = slab(4)
            wgrad[2, 0, :, LANE:ch] = rest[:, 0:hl]
            wgrad[2, 1, :, LANE:ch] = pltpu.roll(rest, hl, 1)[:, 0:hl]
        if p == 2:
            wgrad[2, 2, :, LANE:ch] = slab(4)[:, 0:hl]
        for r in range(3):
            for c in range(3):
                ready = c if r < 2 else max(c, 1)
                if ready == p:
                    store(wgrad.at[r, c], wgrad_hbm.at[r, c])

    nt = ((1,), (1,))
    add_up(0)
    add_up(1)
    over_plane(0)
    add_up(2)
    over_plane(1)
    pass_corners(1)
    over_plane(2)
    spread(1, wide_g, grad.astype(F32), (2, 1, 0))
    back = mm(wide_g[cols : cols + cells, :], k_bwd[1], nt)
    over_z(0)
    finish_halo(1)
    spread_halo(1, wide_g, (2, 1, 0))
    over_z(1)
    back = back + mm(wide_g[0:cells, :], k_bwd[2], nt)
    z_return(0)
    over_z(2)
    z_return(1)
    inner = mm(wide_g[2 * cols : cols + cells, :], k_bwd[0], nt)
    edge = mm(wide_g[cols + cells : 2 * cols + cells, :], k_north[...], nt)
    back = back + jnp.concatenate([inner, edge], axis=0)
    sgrad[...] = jnp.where(keep > 0, back, 0.0).astype(BF16).reshape(sgrad.shape)
    store(sgrad, sgrad_hbm)
    plane_return(0)
    z_return(2)
    plane_return(1)
    plane_return(2)
    core_return(0)
    core_return(1)
    hand_out(0)
    core_return(2)
    hand_out(1)
    hand_out(2)

    finish_sends(0)
    finish_sends(1)
    for q in parts:
        for copy in q["sent"]:
            copy.wait_send()
    for copy in stores:
        copy.wait()


def write_body(out, sgrad, wgrad, out_hbm, sgrad_hbm, wgrad_hbm, sems):
    copies = []
    for src, dst in ((out, out_hbm), (sgrad, sgrad_hbm)):
        step = src.shape[1] // 4
        for k in range(4):
            piece = (0, pl.ds(k * step, step))
            copies.append((src.at[piece], dst.at[piece]))
    for r in range(3):
        for c in range(3):
            copies.append((wgrad.at[r, c], wgrad_hbm.at[r, c]))
    copies = [pltpu.make_async_copy(a, b, sems.at[i]) for i, (a, b) in enumerate(copies)]
    for copy in copies:
        copy.start()
    for copy in copies:
        copy.wait()


def body(states, cotangent, weights, land_mask, ocean_tiles):
    n_lon, n_lat, n_dp = (lax.axis_size(a) for a in ("lon", "lat", "dp"))
    batch, rows, cols, ch = states.shape
    assert batch == 1 and ch == 192 and n_lon % 2 == 0 and cols & (cols - 1) == 0
    cells = rows * cols
    count = batch * n_dp * rows * n_lat * cols * n_lon
    wide = 2 * LANE
    nz, npl = n_lon // 2, n_lat * n_dp
    groups = 2 * npl
    tile = (SUB, LANE)
    vmem = pltpu.VMEM
    dma = pltpu.SemaphoreType.DMA

    def part_scratch(slabs):
        total = -(-slabs * (ch // SUB) // groups) * groups
        half = total // 2
        per = half // npl
        chunk = -(-per // nz)
        most = max(npl, nz)
        return {
            "wf": vmem((total,) + tile, F32),
            "wb": vmem((total,) + tile, BF16),
            "r1": vmem((half,) + tile, BF16),
            "a1": vmem((npl, per) + tile, F32),
            "b1": vmem((npl, per) + tile, BF16),
            "r2": vmem((npl - 1, per) + tile, BF16),
            "a2": vmem((nz * chunk,) + tile, F32),
            "b2": vmem((nz * chunk,) + tile, BF16),
            "r3": vmem((nz - 1, chunk) + tile, BF16),
            "ag": vmem((2, npl, nz * chunk) + tile, BF16),
            "s": dma((6, most)),
            "q": dma((6, most)),
        }

    scratch = [
        vmem(states.shape, BF16),
        vmem(states.shape, BF16),
        vmem(weights.shape, F32),
        vmem(states.shape, BF16),
        vmem(states.shape, BF16),
        vmem(weights.shape, BF16),
        vmem(land_mask.shape, jnp.int32),
        dma((4,)),
        dma((11,)),
        vmem((2, cells, ch), BF16),
        vmem((2, 2 * rows, ch), BF16),
        vmem((2, 2 * rows, ch), BF16),
        vmem((2, 2, cols + 2 * rows, ch), BF16),
        vmem((cells + 2 * cols, 3 * wide), BF16),
        vmem((cells + 2 * cols, 3 * wide), BF16),
        vmem((cells + 2 * cols, 3 * wide), BF16),
        vmem((3, 3 * wide, ch), BF16),
        vmem((3, ch, 3 * wide), BF16),
        vmem((ch, 3 * wide), BF16),
        vmem((3, wide, cells + 2 * cols), BF16),
        [part_scratch(slabs) for slabs in (4, 5, 5)],
        dma((2, 6)), dma((2, 6)),
    ]
    in_hbm = pl.BlockSpec(memory_space=pltpu.HBM)
    geo = (n_lon, n_lat, n_dp, 1.0 / math.sqrt(count))
    results = pl.pallas_call(
        functools.partial(kernel_body, geo),
        out_shape=(
            jax.ShapeDtypeStruct(states.shape, BF16),
            jax.ShapeDtypeStruct(states.shape, BF16),
            jax.ShapeDtypeStruct(weights.shape, F32),
        ),
        in_specs=[in_hbm] * 4 + [pl.BlockSpec(memory_space=pltpu.SMEM)],
        out_specs=(in_hbm,) * 3,
        scratch_shapes=scratch,
        compiler_params=pltpu.CompilerParams(
            collective_id=0, has_side_effects=True, vmem_limit_bytes=60 * 2**20
        ),
        cost_estimate=pl.CostEstimate(
            flops=54 * cells * ch * ch, bytes_accessed=5_000_000, transcendentals=cells * ch
        ),
    )(states, cotangent, weights, land_mask, ocean_tiles)
    return pl.pallas_call(
        write_body,
        out_shape=tuple(jax.ShapeDtypeStruct(v.shape, v.dtype) for v in results),
        in_specs=[in_hbm] * 3,
        out_specs=(in_hbm,) * 3,
        scratch_shapes=[dma((17,))],
        compiler_params=pltpu.CompilerParams(vmem_limit_bytes=60 * 2**20),
    )(*results)


def solution(mesh):
    in_specs = (
        P("dp", "lat", "lon", None),
        P("dp", "lat", "lon", None),
        P(),
        P("lat", "lon"),
        P("lat", "lon", None),
    )
    out_specs = (P("dp", "lat", "lon", None), P("dp", "lat", "lon", None), P())
    return jax.shard_map(body, mesh=mesh, in_specs=in_specs, out_specs=out_specs, check_vma=False)
```

time: 48 us -> 127 us (2.65)
  Pallas kernels: 39.7 us -> 126 us
  local copies, waits for them, and re-layouts: 7.39 us -> 0 us
    pallas_call x0 -> x1, Pallas kernels: none -> 86.6 us  [body(): pl.pallas_call(write_body, out_shape=tuple((jax.ShapeDtypeStruct(v.shape,...]
    unnamed x13 -> x0, local copies, waits for them, and re-layouts: 7.39 us -> none
where the time goes in v2:
time: 127 us
  Pallas kernels  126 us (99%)
    pallas_call x1, Pallas kernels, body(): pl.pallas_call(write_body, out_shape=tuple((jax.ShapeDtypeStruct(v.shape,...  86.6 us
    pallas_call x1, Pallas kernels, body(): pl.pallas_call(functools.partial(kernel_body, geo), out_shape=(jax.ShapeD...  39.3 us

profile of v2, /device:TPU:1, one launch (start us, length us, event | category | flops | bytes accessed | tf_op | source)
XLA Modules:
  0.0 126.6 jit_solution(818520416668954903)
XLA Ops:
  0.6 39.3 %shard_map.76 = (bf16[1,16,64,192]{3,2,1,0:T(8,128)(2,1)}, bf16[1,16,64,192]{3,2,1,0:T(8,128)(2,1)}, f32[3,3,192,192]{3,2,1,0:T(8,128)}) custom-call(bf16[1,16,64,192]{3,2,1,0:T(8,128)(2,1)} %states_hbm.1, bf16[1,16,64,192]{3,2,1,0:T(8,128)(2,1)} %cotangent_hbm.1, bf16[3,3,192,192]{3,2,1,0:T(8,128)(2,1)} %weights_hbm.1, s32[16,64]{1,0:T(8,128)} %land_hbm.1, ...), custom_call_target="tpu_custom_call" | custom-call | flops 2038431744 | bytes 5000000 | tf_op jit(solution)/shard_map/pallas_call | solution.py:562
  39.9 86.6 %shard_map.77 = (bf16[1,16,64,192]{3,2,1,0:T(8,128)(2,1)}, bf16[1,16,64,192]{3,2,1,0:T(8,128)(2,1)}, f32[3,3,192,192]{3,2,1,0:T(8,128)}) custom-call(bf16[1,16,64,192]{3,2,1,0:T(8,128)(2,1)} %get-tuple-element.6.out, bf16[1,16,64,192]{3,2,1,0:T(8,128)(2,1)} %get-tuple-element.7.sgrad, f32[3,3,192,192]{3,2,1,0:T(8,128)} %get-tuple-element.8.wgrad), custom_call_target="tpu_custom_call" | custom-call | tf_op jit(solution)/shard_map/pallas_call | solution.py:579

commit v3 on v2

--- a/solution.py
+++ b/solution.py
@@ -212,7 +212,7 @@
 
     def spread(w, ref, values, order):
         lane = [b * wide for b in order]
-        body = pl.ds(cols, cells)
+        body = pl.ds(0, cells)
         ref[body, lane[1] : lane[1] + ch] = own[w]
         low = mm(first_of, colrecv[w, :rows])
         ref[body, lane[0] : lane[0] + ch] = jnp.where(
@@ -229,7 +229,7 @@
         block = jnp.where(p >= cols, 1, 0) + jnp.where(p >= 2 * cols, 1, 0)
         east = p - cols * block + block - 1
         flip = jnp.where(top, 1, 0)
-        for slot, at in ((NORTH, cells + cols), (SOUTH, 0)):
+        for slot, at in ((NORTH, cells), (SOUTH, cells + cols)):
             if slot == NORTH:
                 e = east + flip * (cols - 1 - 2 * east)
                 edge = flip * (rows - 1)
@@ -250,9 +250,11 @@
         gap = pl.ds(c * wide + LANE, LANE)
         for ref in (wide_x, wide_g, lag_g):
             ref[:, gap] = jnp.zeros((ref.shape[0], LANE), BF16)
-        for lo, hi in ((0, c * cols), (c * cols + cells, cells + 2 * cols)):
-            if hi > lo:
-                lag_g[lo:hi, c * wide : (c + 1) * wide] = jnp.zeros((hi - lo, wide), BF16)
+    for r, lo, hi in (
+        (0, cells - cols, cells + cols), (1, cells, cells + 2 * cols),
+        (2, 0, cols), (2, cells + cols, cells + 2 * cols),
+    ):
+        lag_g[lo:hi, r * wide : (r + 1) * wide] = jnp.zeros((hi - lo, wide), BF16)
     for r in range(3):
         k_bwd[r] = jnp.zeros_like(k_bwd[r])
         k_fwd[r] = jnp.zeros_like(k_fwd[r])
@@ -273,28 +275,50 @@
 
     pass_corners(0)
     spread(0, wide_x, masked, (0, 1, 2))
-    pre = mm(wide_x[cols : cols + cells, :], k_fwd[1])
-    low = mm(wide_x[cols:cells, :], k_fwd[0])
-    high = mm(wide_x[2 * cols : cols + cells, :], k_fwd[2])
+    fetch[3].wait()
+
+    def activate(lo, hi, pre):
+        here = keep[lo:hi]
+        sig = 1.0 / (1.0 + jnp.exp(-pre))
+        first, last = lo // cols, hi // cols
+        shape = (1, last - first, cols, ch)
+        out[:, first:last] = (here * pre * sig).astype(BF16).reshape(shape)
+        slope = sig * (1.0 + pre * (1.0 - sig))
+        upstream = cotangent[:, first:last].reshape(hi - lo, ch).astype(F32)
+        grad = (here * upstream * slope).astype(BF16)
+        own[1, lo:hi] = grad
+        lag_g[lo:hi, wide : wide + ch] = grad
+        for r, step in ((0, -cols), (2, cols)):
+            a, b = lo + step, hi + step
+            if a < 0:
+                lag_g[cells + cols : cells + 2 * cols, 0:ch] = grad[:cols]
+                grad_in, a = grad[cols:], 0
+            elif b > cells:
+                lag_g[cells : cells + cols, 2 * wide : 2 * wide + ch] = grad[hi - lo - cols :]
+                grad_in, b = grad[: hi - lo - cols], cells
+            else:
+                grad_in = grad
+            if b > a:
+                lag_g[a:b, r * wide : r * wide + ch] = grad_in
+
+    for c in range(3):
+        x_turned[c, :, 0:cells] = wide_x[0:cells, c * wide : (c + 1) * wide].T
+    pre = mm(wide_x[0:cells, :], k_fwd[1])
+    low = mm(wide_x[0 : cells - cols, :], k_fwd[0])
+    high = mm(wide_x[cols:cells, :], k_fwd[2])
+    mid = slice(cols, cells - cols)
+    activate(cols, cells - cols, pre[mid] + low[: cells - 2 * cols] + high[cols:])
     finish_halo(0)
     spread_halo(0, wide_x, (0, 1, 2))
-    low_edge = mm(wide_x[0:cols, :], k_fwd[0])
-    high_edge = mm(wide_x[cells + cols :, :], k_fwd[2])
-    pre = pre + jnp.concatenate([low_edge, low], axis=0)
-    pre = pre + jnp.concatenate([high, high_edge], axis=0)
-    fetch[3].wait()
     for c in range(3):
-        x_turned[c] = wide_x[:, c * wide : (c + 1) * wide].T
-    sig = 1.0 / (1.0 + jnp.exp(-pre))
-    out[...] = (keep * pre * sig).astype(BF16).reshape(out.shape)
-    store(out, out_hbm)
-    slope = sig * (1.0 + pre * (1.0 - sig))
-    grad = (keep * cotangent[...].reshape(cells, ch).astype(F32) * slope).astype(BF16)
-    own[1] = grad
-    for r in range(3):
-        lag_g[r * cols : r * cols + cells, r * wide : r * wide + ch] = grad
+        x_turned[c, :, cells:] = wide_x[cells:, c * wide : (c + 1) * wide].T
+    low_edge = mm(wide_x[cells + cols :, :], k_fwd[0])
+    high_edge = mm(wide_x[cells : cells + cols, :], k_fwd[2])
+    activate(0, cols, pre[:cols] + high[:cols] + low_edge)
+    activate(cells - cols, cells, pre[cells - cols :] + low[cells - 2 * cols :] + high_edge)
     colsend[1] = mm(pick, own[1]).astype(BF16)
     start_first(1)
+    store(out, out_hbm)
 
     units = ch // SUB
     hl = LANE // 2
@@ -447,18 +471,20 @@
     over_plane(1)
     pass_corners(1)
     over_plane(2)
-    spread(1, wide_g, grad.astype(F32), (2, 1, 0))
-    back = mm(wide_g[cols : cols + cells, :], k_bwd[1], nt)
+    spread(1, wide_g, own[1].astype(F32), (2, 1, 0))
+    back = mm(wide_g[0:cells, :], k_bwd[1], nt)
     over_z(0)
     finish_halo(1)
     spread_halo(1, wide_g, (2, 1, 0))
     over_z(1)
-    back = back + mm(wide_g[0:cells, :], k_bwd[2], nt)
+    below = mm(wide_g[0 : cells - cols, :], k_bwd[2], nt)
+    below_edge = mm(wide_g[cells + cols :, :], k_bwd[2], nt)
+    back = back + jnp.concatenate([below_edge, below], axis=0)
     z_return(0)
     over_z(2)
     z_return(1)
-    inner = mm(wide_g[2 * cols : cols + cells, :], k_bwd[0], nt)
-    edge = mm(wide_g[cols + cells : 2 * cols + cells, :], k_north[...], nt)
+    inner = mm(wide_g[cols:cells, :], k_bwd[0], nt)
+    edge = mm(wide_g[cells : cells + cols, :], k_north[...], nt)
     back = back + jnp.concatenate([inner, edge], axis=0)
     sgrad[...] = jnp.where(keep > 0, back, 0.0).astype(BF16).reshape(sgrad.shape)
     store(sgrad, sgrad_hbm)
@@ -482,20 +508,24 @@
         copy.wait()
 
 
-def write_body(out, sgrad, wgrad, out_hbm, sgrad_hbm, wgrad_hbm, sems):
-    copies = []
-    for src, dst in ((out, out_hbm), (sgrad, sgrad_hbm)):
+def write_body(out, sgrad, wgrad, out_hbm, sgrad_hbm, wgrad_hbm, a, b, c, load, save):
+    steps = []
+    for src, mid, dst in ((out, a, out_hbm), (sgrad, b, sgrad_hbm)):
         step = src.shape[1] // 4
         for k in range(4):
             piece = (0, pl.ds(k * step, step))
-            copies.append((src.at[piece], dst.at[piece]))
+            steps.append((src.at[piece], mid.at[piece], dst.at[piece]))
     for r in range(3):
-        for c in range(3):
-            copies.append((wgrad.at[r, c], wgrad_hbm.at[r, c]))
-    copies = [pltpu.make_async_copy(a, b, sems.at[i]) for i, (a, b) in enumerate(copies)]
-    for copy in copies:
+        for k in range(3):
+            steps.append((wgrad.at[r, k], c.at[r, k], wgrad_hbm.at[r, k]))
+    loads = [pltpu.make_async_copy(x, y, load.at[i]) for i, (x, y, _) in enumerate(steps)]
+    saves = [pltpu.make_async_copy(y, w, save.at[i]) for i, (_, y, w) in enumerate(steps)]
+    for copy in loads:
         copy.start()
-    for copy in copies:
+    for arrive, leave in zip(loads, saves):
+        arrive.wait()
+        leave.start()
+    for copy in saves:
         copy.wait()
 
 
@@ -581,7 +611,7 @@
         out_shape=tuple(jax.ShapeDtypeStruct(v.shape, v.dtype) for v in results),
         in_specs=[in_hbm] * 3,
         out_specs=(in_hbm,) * 3,
-        scratch_shapes=[dma((17,))],
+        scratch_shapes=[vmem(v.shape, v.dtype) for v in results] + [dma((17,)), dma((17,))],
         compiler_params=pltpu.CompilerParams(vmem_limit_bytes=60 * 2**20),
     )(*results)
 

time: 127 us -> 41.2 us (0.32)
  Pallas kernels: 126 us -> 40.3 us
    pallas_call x1, Pallas kernels: 86.6 us -> 2.84 us  [body(): pl.pallas_call(write_body, out_shape=tuple((jax.ShapeDtypeStruct(v.shape,...]
    pallas_call x1, Pallas kernels: 39.3 us -> 37.5 us  [body(): pl.pallas_call(functools.partial(kernel_body, geo), out_shape=(jax.ShapeD...]
where the time goes in v3:
time: 41.2 us; the launch traced here: 41 us
  Pallas kernels  40.3 us (98%)
  between operations  0.64 us (2%)
    pallas_call x1, Pallas kernels, body(): pl.pallas_call(functools.partial(kernel_body, geo), out_shape=(jax.ShapeD...  37.5 us
    pallas_call x1, Pallas kernels, body(): pl.pallas_call(write_body, out_shape=tuple((jax.ShapeDtypeStruct(v.shape,...  2.84 us

profile of v3, /device:TPU:1, one launch (start us, length us, event | category | flops | bytes accessed | tf_op | source)
XLA Modules:
  0.0 41.0 jit_solution(18285824529326841690)
XLA Ops:
  0.6 37.5 %shard_map.76 = (bf16[1,16,64,192]{3,2,1,0:T(8,128)(2,1)}, bf16[1,16,64,192]{3,2,1,0:T(8,128)(2,1)}, f32[3,3,192,192]{3,2,1,0:T(8,128)}) custom-call(bf16[1,16,64,192]{3,2,1,0:T(8,128)(2,1)} %states_hbm.1, bf16[1,16,64,192]{3,2,1,0:T(8,128)(2,1)} %cotangent_hbm.1, bf16[3,3,192,192]{3,2,1,0:T(8,128)(2,1)} %weights_hbm.1, s32[16,64]{1,0:T(8,128)} %land_hbm.1, ...), custom_call_target="tpu_custom_call" | custom-call | flops 2038431744 | bytes 5000000 | tf_op jit(solution)/shard_map/pallas_call | solution.py:592
  38.1 2.8 %shard_map.77 = (bf16[1,16,64,192]{3,2,1,0:T(8,128)(2,1)}, bf16[1,16,64,192]{3,2,1,0:T(8,128)(2,1)}, f32[3,3,192,192]{3,2,1,0:T(8,128)}) custom-call(bf16[1,16,64,192]{3,2,1,0:T(8,128)(2,1)} %get-tuple-element.6.out, bf16[1,16,64,192]{3,2,1,0:T(8,128)(2,1)} %get-tuple-element.7.sgrad, f32[3,3,192,192]{3,2,1,0:T(8,128)} %get-tuple-element.8.wgrad), custom_call_target="tpu_custom_call" | custom-call | tf_op jit(solution)/shard_map/pallas_call | solution.py:609

commit v4 on v3

--- a/solution.py
+++ b/solution.py
@@ -31,9 +31,9 @@
 
 def kernel_body(
     geo,
-    states_hbm, cotangent_hbm, weights_hbm, land_hbm, tiles,
-    out_hbm, sgrad_hbm, wgrad_hbm,
-    out, sgrad, wgrad, states, cotangent, weights, land, in_sem, out_sem,
+    states_hbm, cotangent_hbm, weights_hbm, land_hbm, tiles_hbm,
+    out, sgrad, wgrad,
+    states, cotangent, weights, land, tiles, in_sem,
     own, colsend, colrecv, halo, wide_x, wide_g, lag_g, k_fwd, k_bwd, k_north,
     x_turned, parts, hs_send, hs_recv,
 ):
@@ -74,18 +74,11 @@
     fetch = []
     for i, (src, dst) in enumerate((
         (land_hbm, land), (states_hbm, states), (weights_hbm, weights),
-        (cotangent_hbm, cotangent),
+        (cotangent_hbm, cotangent), (tiles_hbm, tiles),
     )):
         copy = pltpu.make_async_copy(src, dst, in_sem.at[i])
         copy.start()
         fetch.append(copy)
-    stores = []
-
-    def store(src, dst):
-        copy = pltpu.make_async_copy(src, dst, out_sem.at[len(stores)])
-        copy.start()
-        stores.append(copy)
-
     barrier = pltpu.get_barrier_semaphore()
 
     def greet(where):
@@ -104,20 +97,17 @@
 
     tile_cols = cols // TS
     number = iota((rows, cols), 0) // TS * tile_cols + iota((rows, cols), 1) // TS
-    hit = number == tiles[0, 0, 0]
+    fetch[0].wait()
+    fetch[4].wait()
+    hit = number == tiles[0, :, 0:1]
     for slot in range(1, tiles.shape[2]):
-        hit = hit | (number == tiles[0, 0, slot])
-    fetch[0].wait()
+        hit = hit | (number == tiles[0, :, slot : slot + 1])
     keep_plane = jnp.where(hit, land[...], 0).astype(F32).astype(BF16)
     cell = iota((cells, rows), 0) - cols * iota((cells, rows), 1)
     by_row = mm(onehot((cell >= 0) & (cell < cols)), keep_plane)
     pos = iota((cells, cols), 0) & (cols - 1)
     by_cell = jnp.where(pos == iota((cells, cols), 1), by_row, 0.0).astype(BF16)
     keep = mm(by_cell, jnp.ones((cols, ch), BF16))
-    column = iota((cells, ch), 0) & (cols - 1)
-    at_first, at_last = column == 0, column == cols - 1
-    first_of = onehot(cell == 0)
-    last_of = onehot(cell == cols - 1)
     pick = iota((2 * rows, cells), 1) - jnp.where(
         iota((2 * rows, cells), 0) < rows,
         cols * iota((2 * rows, cells), 0),
@@ -214,14 +204,20 @@
         lane = [b * wide for b in order]
         body = pl.ds(0, cells)
         ref[body, lane[1] : lane[1] + ch] = own[w]
-        low = mm(first_of, colrecv[w, :rows])
-        ref[body, lane[0] : lane[0] + ch] = jnp.where(
-            at_first, low, pltpu.roll(values, 1, 0)
-        ).astype(BF16)
-        high = mm(last_of, colrecv[w, rows:])
-        ref[body, lane[2] : lane[2] + ch] = jnp.where(
-            at_last, high, pltpu.roll(values, cells - 1, 0)
-        ).astype(BF16)
+        ref[body, lane[0] : lane[0] + ch] = pltpu.roll(values, 1, 0).astype(BF16)
+        ref[body, lane[2] : lane[2] + ch] = pltpu.roll(values, cells - 1, 0).astype(BF16)
+
+    def patch(w, ref, order):
+        line = iota((SUB, ch), 0)
+        margin = colrecv[w].astype(F32)
+        for j in range(rows):
+            for b, at, spot in ((0, j * cols, 0), (2, (j + 1) * cols - SUB, SUB - 1)):
+                lane = order[b] * wide
+                here = (slice(at, at + SUB), slice(lane, lane + ch))
+                value = margin[j + (rows if b else 0)][None]
+                ref[here] = jnp.where(
+                    line == spot, value, ref[here].astype(F32)
+                ).astype(BF16)
 
     def spread_halo(w, ref, order):
         shape = (3 * cols, cols + 2 * rows)
@@ -257,7 +253,8 @@
         lag_g[lo:hi, r * wide : (r + 1) * wide] = jnp.zeros((hi - lo, wide), BF16)
     for r in range(3):
         k_bwd[r] = jnp.zeros_like(k_bwd[r])
-        k_fwd[r] = jnp.zeros_like(k_fwd[r])
+        for c in range(3):
+            k_fwd[r, c * wide + ch : (c + 1) * wide, :] = jnp.zeros((wide - ch, ch), BF16)
     for r in range(3):
         for c in range(3):
             k_fwd[r, c * wide : c * wide + ch, :] = weights[r, c]
@@ -273,13 +270,14 @@
         for c in range(3):
             k_north[:, c * wide : c * wide + ch] = weights[0, c]
 
+    spread(0, wide_x, masked, (0, 1, 2))
     pass_corners(0)
-    spread(0, wide_x, masked, (0, 1, 2))
+    patch(0, wide_x, (0, 1, 2))
     fetch[3].wait()
 
     def activate(lo, hi, pre):
         here = keep[lo:hi]
-        sig = 1.0 / (1.0 + jnp.exp(-pre))
+        sig = 0.5 * jnp.tanh(0.5 * pre) + 0.5
         first, last = lo // cols, hi // cols
         shape = (1, last - first, cols, ch)
         out[:, first:last] = (here * pre * sig).astype(BF16).reshape(shape)
@@ -318,7 +316,6 @@
     activate(cells - cols, cells, pre[cells - cols :] + low[cells - 2 * cols :] + high_edge)
     colsend[1] = mm(pick, own[1]).astype(BF16)
     start_first(1)
-    store(out, out_hbm)
 
     units = ch // SUB
     hl = LANE // 2
@@ -457,11 +454,6 @@
             wgrad[2, 1, :, LANE:ch] = pltpu.roll(rest, hl, 1)[:, 0:hl]
         if p == 2:
             wgrad[2, 2, :, LANE:ch] = slab(4)[:, 0:hl]
-        for r in range(3):
-            for c in range(3):
-                ready = c if r < 2 else max(c, 1)
-                if ready == p:
-                    store(wgrad.at[r, c], wgrad_hbm.at[r, c])
 
     nt = ((1,), (1,))
     add_up(0)
@@ -470,8 +462,9 @@
     add_up(2)
     over_plane(1)
     pass_corners(1)
+    spread(1, wide_g, own[1].astype(F32), (2, 1, 0))
     over_plane(2)
-    spread(1, wide_g, own[1].astype(F32), (2, 1, 0))
+    patch(1, wide_g, (2, 1, 0))
     back = mm(wide_g[0:cells, :], k_bwd[1], nt)
     over_z(0)
     finish_halo(1)
@@ -487,7 +480,6 @@
     edge = mm(wide_g[cells : cells + cols, :], k_north[...], nt)
     back = back + jnp.concatenate([inner, edge], axis=0)
     sgrad[...] = jnp.where(keep > 0, back, 0.0).astype(BF16).reshape(sgrad.shape)
-    store(sgrad, sgrad_hbm)
     plane_return(0)
     z_return(2)
     plane_return(1)
@@ -504,27 +496,21 @@
     for q in parts:
         for copy in q["sent"]:
             copy.wait_send()
-    for copy in stores:
-        copy.wait()
-
-
-def write_body(out, sgrad, wgrad, out_hbm, sgrad_hbm, wgrad_hbm, a, b, c, load, save):
+
+
+def write_body(out, sgrad, wgrad, out_hbm, sgrad_hbm, wgrad_hbm, save):
     steps = []
-    for src, mid, dst in ((out, a, out_hbm), (sgrad, b, sgrad_hbm)):
+    for src, dst in ((out, out_hbm), (sgrad, sgrad_hbm)):
         step = src.shape[1] // 4
         for k in range(4):
             piece = (0, pl.ds(k * step, step))
-            steps.append((src.at[piece], mid.at[piece], dst.at[piece]))
+            steps.append((src.at[piece], dst.at[piece]))
     for r in range(3):
         for k in range(3):
-            steps.append((wgrad.at[r, k], c.at[r, k], wgrad_hbm.at[r, k]))
-    loads = [pltpu.make_async_copy(x, y, load.at[i]) for i, (x, y, _) in enumerate(steps)]
-    saves = [pltpu.make_async_copy(y, w, save.at[i]) for i, (_, y, w) in enumerate(steps)]
-    for copy in loads:
+            steps.append((wgrad.at[r, k], wgrad_hbm.at[r, k]))
+    saves = [pltpu.make_async_copy(y, w, save.at[i]) for i, (y, w) in enumerate(steps)]
+    for copy in saves:
         copy.start()
-    for arrive, leave in zip(loads, saves):
-        arrive.wait()
-        leave.start()
     for copy in saves:
         copy.wait()
 
@@ -566,13 +552,10 @@
     scratch = [
         vmem(states.shape, BF16),
         vmem(states.shape, BF16),
-        vmem(weights.shape, F32),
-        vmem(states.shape, BF16),
-        vmem(states.shape, BF16),
         vmem(weights.shape, BF16),
         vmem(land_mask.shape, jnp.int32),
-        dma((4,)),
-        dma((11,)),
+        vmem(ocean_tiles.shape, jnp.int32),
+        dma((5,)),
         vmem((2, cells, ch), BF16),
         vmem((2, 2 * rows, ch), BF16),
         vmem((2, 2 * rows, ch), BF16),
@@ -587,32 +570,37 @@
         [part_scratch(slabs) for slabs in (4, 5, 5)],
         dma((2, 6)), dma((2, 6)),
     ]
+    in_vmem = pl.BlockSpec(memory_space=pltpu.VMEM)
     in_hbm = pl.BlockSpec(memory_space=pltpu.HBM)
     geo = (n_lon, n_lat, n_dp, 1.0 / math.sqrt(count))
+    pinned = [
+        pltpu.with_memory_space_constraint(v, pltpu.HBM)
+        for v in (states, cotangent, weights, land_mask, ocean_tiles)
+    ]
     results = pl.pallas_call(
         functools.partial(kernel_body, geo),
         out_shape=(
-            jax.ShapeDtypeStruct(states.shape, BF16),
-            jax.ShapeDtypeStruct(states.shape, BF16),
-            jax.ShapeDtypeStruct(weights.shape, F32),
+            vmem(states.shape, BF16),
+            vmem(states.shape, BF16),
+            vmem(weights.shape, F32),
         ),
-        in_specs=[in_hbm] * 4 + [pl.BlockSpec(memory_space=pltpu.SMEM)],
-        out_specs=(in_hbm,) * 3,
+        in_specs=[in_hbm] * 5,
+        out_specs=(in_vmem,) * 3,
         scratch_shapes=scratch,
         compiler_params=pltpu.CompilerParams(
-            collective_id=0, has_side_effects=True, vmem_limit_bytes=60 * 2**20
+            collective_id=0, has_side_effects=True, vmem_limit_bytes=40 * 2**20
         ),
         cost_estimate=pl.CostEstimate(
             flops=54 * cells * ch * ch, bytes_accessed=5_000_000, transcendentals=cells * ch
         ),
-    )(states, cotangent, weights, land_mask, ocean_tiles)
+    )(*pinned)
     return pl.pallas_call(
         write_body,
         out_shape=tuple(jax.ShapeDtypeStruct(v.shape, v.dtype) for v in results),
-        in_specs=[in_hbm] * 3,
+        in_specs=[in_vmem] * 3,
         out_specs=(in_hbm,) * 3,
-        scratch_shapes=[vmem(v.shape, v.dtype) for v in results] + [dma((17,)), dma((17,))],
-        compiler_params=pltpu.CompilerParams(vmem_limit_bytes=60 * 2**20),
+        scratch_shapes=[dma((17,))],
+        compiler_params=pltpu.CompilerParams(vmem_limit_bytes=2**20),
     )(*results)
 
 

time: 41.2 us -> 38.5 us (0.934)
  Pallas kernels: 40.3 us -> 37.6 us
    pallas_call x1, Pallas kernels: 37.5 us -> 36 us  [body(): pl.pallas_call(functools.partial(kernel_body, geo), out_shape=(vmem(state...]
    pallas_call x1, Pallas kernels: 2.84 us -> 1.69 us  [body(): pl.pallas_call(write_body, out_shape=tuple((jax.ShapeDtypeStruct(v.shape,...]
where the time goes in v4:
time: 38.5 us; the launch traced here: 38.3 us
  Pallas kernels  37.6 us (98%)
  between operations  0.64 us (2%)
    pallas_call x1, Pallas kernels, body(): pl.pallas_call(functools.partial(kernel_body, geo), out_shape=(vmem(state...  36 us
    pallas_call x1, Pallas kernels, body(): pl.pallas_call(write_body, out_shape=tuple((jax.ShapeDtypeStruct(v.shape,...  1.69 us

profile of v4, /device:TPU:1, one launch (start us, length us, event | category | flops | bytes accessed | tf_op | source)
XLA Modules:
  0.0 38.3 jit_solution(13447146979635803287)
XLA Ops:
  0.6 36.0 %shard_map.76 = (bf16[1,16,64,192]{3,2,1,0:T(8,128)(2,1)S(1)}, bf16[1,16,64,192]{3,2,1,0:T(8,128)(2,1)S(1)}, f32[3,3,192,192]{3,2,1,0:T(8,128)S(1)}) custom-call(bf16[1,16,64,192]{3,2,1,0:T(8,128)(2,1)} %states_hbm.1, bf16[1,16,64,192]{3,2,1,0:T(8,128)(2,1)} %cotangent_hbm.1, bf16[3,3,192,192]{3,2,1,0:T(8,128)(2,1)} %weights_hbm.1, s32[16,64]{1,0:T(8,128)} %land_hbm.1, ...), custom_call_target="tpu_custom_call" | custom-call | flops 2038431744 | bytes 5000000 | tf_op jit(solution)/shard_map/pallas_call | solution.py:580
  36.6 1.7 %shard_map.77 = (bf16[1,16,64,192]{3,2,1,0:T(8,128)(2,1)}, bf16[1,16,64,192]{3,2,1,0:T(8,128)(2,1)}, f32[3,3,192,192]{3,2,1,0:T(8,128)}) custom-call(bf16[1,16,64,192]{3,2,1,0:T(8,128)(2,1)S(1)} %get-tuple-element.6.out, bf16[1,16,64,192]{3,2,1,0:T(8,128)(2,1)S(1)} %get-tuple-element.7.sgrad, f32[3,3,192,192]{3,2,1,0:T(8,128)S(1)} %get-tuple-element.8.wgrad), custom_call_target="tpu_custom_call" | custom-call | tf_op jit(solution)/shard_map/pallas_call | solution.py:597

commit v5 on v4

--- a/solution.py
+++ b/solution.py
@@ -73,8 +73,8 @@
 
     fetch = []
     for i, (src, dst) in enumerate((
-        (land_hbm, land), (states_hbm, states), (weights_hbm, weights),
-        (cotangent_hbm, cotangent), (tiles_hbm, tiles),
+        (land_hbm, land), (tiles_hbm, tiles), (states_hbm, states),
+        (weights_hbm, weights), (cotangent_hbm, cotangent),
     )):
         copy = pltpu.make_async_copy(src, dst, in_sem.at[i])
         copy.start()
@@ -97,25 +97,25 @@
 
     tile_cols = cols // TS
     number = iota((rows, cols), 0) // TS * tile_cols + iota((rows, cols), 1) // TS
-    fetch[0].wait()
-    fetch[4].wait()
-    hit = number == tiles[0, :, 0:1]
-    for slot in range(1, tiles.shape[2]):
-        hit = hit | (number == tiles[0, :, slot : slot + 1])
-    keep_plane = jnp.where(hit, land[...], 0).astype(F32).astype(BF16)
     cell = iota((cells, rows), 0) - cols * iota((cells, rows), 1)
-    by_row = mm(onehot((cell >= 0) & (cell < cols)), keep_plane)
-    pos = iota((cells, cols), 0) & (cols - 1)
-    by_cell = jnp.where(pos == iota((cells, cols), 1), by_row, 0.0).astype(BF16)
-    keep = mm(by_cell, jnp.ones((cols, ch), BF16))
+    in_row = onehot((cell >= 0) & (cell < cols))
     pick = iota((2 * rows, cells), 1) - jnp.where(
         iota((2 * rows, cells), 0) < rows,
         cols * iota((2 * rows, cells), 0),
         cols * (iota((2 * rows, cells), 0) - rows) + cols - 1,
     )
     pick = onehot(pick == 0)
-
+    fetch[0].wait()
     fetch[1].wait()
+    hit = number == tiles[0, :, 0:1]
+    for slot in range(1, tiles.shape[2]):
+        hit = hit | (number == tiles[0, :, slot : slot + 1])
+    keep_plane = jnp.where(hit, land[...], 0).astype(F32).astype(BF16)
+    by_row = mm(in_row, keep_plane)
+    pos = iota((cells, cols), 0) & (cols - 1)
+    by_cell = jnp.where(pos == iota((cells, cols), 1), by_row, 0.0).astype(BF16)
+    keep = mm(by_cell, jnp.ones((cols, ch), BF16))
+    fetch[2].wait()
     masked = jnp.where(keep > 0, states[...].reshape(cells, ch).astype(F32), 0.0)
     own[0] = masked.astype(BF16)
     colsend[0] = mm(pick, own[0]).astype(BF16)
@@ -240,7 +240,7 @@
                 ]
 
     start_first(0)
-    fetch[2].wait()
+    fetch[3].wait()
     k_north[...] = jnp.zeros_like(k_north)
     for c in range(3):
         gap = pl.ds(c * wide + LANE, LANE)
@@ -273,7 +273,7 @@
     spread(0, wide_x, masked, (0, 1, 2))
     pass_corners(0)
     patch(0, wide_x, (0, 1, 2))
-    fetch[3].wait()
+    fetch[4].wait()
 
     def activate(lo, hi, pre):
         here = keep[lo:hi]

time: 38.5 us -> 38.5 us (level)
  no operation moved by 1% of the time
where the time goes in v5:
time: 38.5 us; the launch traced here: 38.3 us
  Pallas kernels  37.6 us (98%)
  between operations  0.64 us (2%)
    pallas_call x1, Pallas kernels, body(): pl.pallas_call(functools.partial(kernel_body, geo), out_shape=(vmem(state...  36 us
    pallas_call x1, Pallas kernels, body(): pl.pallas_call(write_body, out_shape=tuple((jax.ShapeDtypeStruct(v.shape,...  1.69 us

profile of v5, /device:TPU:1, one launch (start us, length us, event | category | flops | bytes accessed | tf_op | source)
XLA Modules:
  0.0 38.3 jit_solution(5337065406246181014)
XLA Ops:
  0.6 36.0 %shard_map.76 = (bf16[1,16,64,192]{3,2,1,0:T(8,128)(2,1)S(1)}, bf16[1,16,64,192]{3,2,1,0:T(8,128)(2,1)S(1)}, f32[3,3,192,192]{3,2,1,0:T(8,128)S(1)}) custom-call(bf16[1,16,64,192]{3,2,1,0:T(8,128)(2,1)} %states_hbm.1, bf16[1,16,64,192]{3,2,1,0:T(8,128)(2,1)} %cotangent_hbm.1, bf16[3,3,192,192]{3,2,1,0:T(8,128)(2,1)} %weights_hbm.1, s32[16,64]{1,0:T(8,128)} %land_hbm.1, ...), custom_call_target="tpu_custom_call" | custom-call | flops 2038431744 | bytes 5000000 | tf_op jit(solution)/shard_map/pallas_call | solution.py:580
  36.6 1.7 %shard_map.77 = (bf16[1,16,64,192]{3,2,1,0:T(8,128)(2,1)}, bf16[1,16,64,192]{3,2,1,0:T(8,128)(2,1)}, f32[3,3,192,192]{3,2,1,0:T(8,128)}) custom-call(bf16[1,16,64,192]{3,2,1,0:T(8,128)(2,1)S(1)} %get-tuple-element.6.out, bf16[1,16,64,192]{3,2,1,0:T(8,128)(2,1)S(1)} %get-tuple-element.7.sgrad, f32[3,3,192,192]{3,2,1,0:T(8,128)S(1)} %get-tuple-element.8.wgrad), custom_call_target="tpu_custom_call" | custom-call | tf_op jit(solution)/shard_map/pallas_call | solution.py:597
